TPU v7x, 32 devices: a whole 2x2x4 slice. The times are simulated.
32 devices in a mesh: grp: 4 (over z), dev: 8 (over y, x, core).
Axes of the slice: x: 2, y: 2, z: 4, core: 2. Of those that a mesh axis runs over, the one named last changes fastest.
Arguments:
- series: float32 [2, 4194304], P(None, ('grp', 'dev')), may hold values from -6 to 6
Outputs:
- spectrum: float32 [2, 4194304], P(None, ('grp', 'dev'))
All inputs are finite; a program needn't handle non-finite values.
Results may differ from a plain program's by a relative error of at most 0.00007.
Values sent between devices are 32-bit elements; how exact they have to be, the bound alone decides.
No kernel may reach another device: no remote copies, remote signals or barrier semaphores. Data moves between devices by JAX's collectives and lax.ppermute only.
A program may use at most 128 MiB of HBM per device.

v0:
```python
import functools
import math

import jax
import jax.numpy as jnp
import numpy as np
from jax import lax
from jax.experimental import pallas as pl
from jax.experimental.pallas import tpu as pltpu
from jax.sharding import PartitionSpec as P

LANES = 128
SUB = 8
AXES = ("grp", "dev")
ORDER = ("dev", "grp")


def roots(product, modulus):
    angle = np.asarray(product, np.int64) % modulus * (-2.0 * math.pi / modulus)
    return np.cos(angle), np.sin(angle)


def times_root(value, k, n):
    re, im = value
    k %= n
    if k == 0:
        return value
    if 4 * k == n:
        return im, -re
    if 2 * k == n:
        return -re, -im
    if 4 * k == 3 * n:
        return -im, re
    if 8 * k == n:
        half = np.float32(math.sqrt(0.5))
        return (re + im) * half, (im - re) * half
    if 8 * k == 3 * n:
        half = np.float32(math.sqrt(0.5))
        return (im - re) * half, (re + im) * -half
    angle = -2.0 * math.pi * k / n
    c, s = np.float32(math.cos(angle)), np.float32(math.sin(angle))
    return re * c - im * s, re * s + im * c


def dft_list(values):
    n = len(values)
    if n == 1:
        return values
    even, odd = dft_list(values[0::2]), dft_list(values[1::2])
    low, high = [], []
    for k in range(n // 2):
        (er, ei), (tr, ti) = even[k], times_root(odd[k], k, n)
        low.append((er + tr, ei + ti))
        high.append((er - tr, ei - ti))
    return low + high


def across_kernel(sources, place_ref, turn_ref, step_ref, in_ref, out_ref):
    count = len(sources)
    rows = in_ref.shape[0] // count // 2
    for j in range(0, rows, SUB):
        take = min(SUB, rows - j)
        values = []
        for at in sources:
            base = (at * rows + j) * 2
            values.append((in_ref[pl.ds(base, take, 2), :], in_ref[pl.ds(base + 1, take, 2), :]))
        for k, (re, im) in enumerate(dft_list(values)):
            base = k * 2 * rows + j
            tc, ts = turn_ref[base : base + take, :], turn_ref[base + rows : base + rows + take, :]
            dc, ds = step_ref[0, 2 * k], step_ref[0, 2 * k + 1]
            c, s = tc * dc - ts * ds, tc * ds + ts * dc
            out_ref[base : base + take, :] = re * c - im * s
            out_ref[base + rows : base + rows + take, :] = re * s + im * c


def across(received, sources, points, scale):
    count = len(sources)
    slab = points // count
    piece = slab // count
    digits = np.arange(count)
    tc, ts = roots(digits[:, None] * np.arange(piece)[None, :], points)
    turn = np.stack([tc, ts], 1).reshape(count * 2 * piece // LANES, LANES) * scale
    dc, ds = roots(digits[:, None] * digits[None, :], count * count)
    step = np.stack([dc, ds], 2).reshape(count, 1, 2 * count)
    place = lax.axis_index(ORDER).astype(jnp.int32).reshape(1)
    whole = pl.BlockSpec(received.shape, lambda i, place: (0, 0))
    return pl.pallas_call(
        functools.partial(across_kernel, sources),
        grid_spec=pltpu.PrefetchScalarGridSpec(
            num_scalar_prefetch=1,
            grid=(1,),
            in_specs=[
                whole,
                pl.BlockSpec((None, 1, 2 * count), lambda i, place: (place[0], 0, 0), memory_space=pltpu.SMEM),
                whole,
            ],
            out_specs=whole,
        ),
        out_shape=jax.ShapeDtypeStruct(received.shape, jnp.float32),
        compiler_params=pltpu.CompilerParams(vmem_limit_bytes=32 << 20),
    )(place, turn.astype(np.float32), step.astype(np.float32), received)


def split_bf16(values):
    high = values.astype(jnp.bfloat16)
    return high, (values - high.astype(jnp.float32)).astype(jnp.bfloat16)


def lane_stage(outer, inner, turn_ref, fh_ref, fl_ref, out_ref, first, second):
    span = outer * inner
    fold = outer // SUB
    for v in range(fold):
        values = []
        for j in range(inner):
            base = v * inner + j
            values.append(
                (
                    first[pl.ds(base, SUB, fold * inner), :],
                    first[pl.ds(span + base, SUB, fold * inner), :],
                )
            )
        for k, (re, im) in enumerate(dft_list(values)):
            base = (v * inner + k) * SUB
            c, s = turn_ref[base : base + SUB, :], turn_ref[span + base : span + base + SUB, :]
            second[base : base + SUB, :LANES] = re * c - im * s
            second[base : base + SUB, LANES:] = re * s + im * c
    xh, xl = split_bf16(second[...])
    dot = functools.partial(
        lax.dot_general, dimension_numbers=(((1,), (1,)), ((), ())), preferred_element_type=jnp.float32
    )
    result = dot(fh_ref[...], xh) + (dot(fh_ref[...], xl) + dot(fl_ref[...], xh))
    for t in range(span // LANES):
        tile = result[:, t * LANES : (t + 1) * LANES]
        out_ref[:, t * SUB : (t + 1) * SUB, :] = tile.reshape(tile.shape[0] // SUB, SUB, LANES)


def local_kernel(piece_rows, mid_ref, turn_ref, fh_ref, fl_ref, in_ref, out_ref, first, second):
    inner = piece_rows
    outer = in_ref.shape[0] // 2 // inner
    span = outer * inner
    for j in range(0, inner, SUB):
        take = min(SUB, inner - j)
        values = []
        for e in range(outer):
            base = e * 2 * inner + j
            values.append((in_ref[base : base + take, :], in_ref[base + inner : base + inner + take, :]))
        for k, (re, im) in enumerate(dft_list(values)):
            base = k * inner + j
            c, s = mid_ref[base : base + take, :], mid_ref[span + base : span + base + take, :]
            first[base : base + take, :] = re * c - im * s
            first[span + base : span + base + take, :] = re * s + im * c
    lane_stage(outer, inner, turn_ref, fh_ref, fl_ref, out_ref, first, second)


def local_tables(outer, inner, lane_rows):
    span = outer * inner
    slab = span * LANES
    mc, ms = roots(np.arange(outer)[:, None] * np.arange(inner)[None, :], span)
    mid = np.broadcast_to(np.stack([mc, ms]).reshape(2 * span, 1), (2 * span, LANES))
    fold = outer // SUB
    v, k, i = np.meshgrid(np.arange(fold), np.arange(inner), np.arange(SUB), indexing="ij")
    kept = ((v + fold * i) + outer * k).reshape(span)
    tc, ts = roots(kept[:, None] * np.arange(LANES)[None, :], slab)
    turn = np.concatenate([tc, ts])
    freq, imag = lane_rows
    fc, fs = roots(freq[:, None] * np.arange(LANES)[None, :], LANES)
    lane = np.where(imag[:, None], np.concatenate([fs, fc], 1), np.concatenate([fc, -fs], 1)).astype(np.float32)
    fh = lane.astype(jnp.bfloat16)
    fl = (lane - fh.astype(np.float32)).astype(jnp.bfloat16)
    return mid.astype(np.float32), turn.astype(np.float32), fh, fl, kept


def local_transform(arrived, outer, inner, lane_rows):
    span = outer * inner
    mid, turn, fh, fl, kept = local_tables(outer, inner, lane_rows)
    return pl.pallas_call(
        functools.partial(local_kernel, inner),
        out_shape=jax.ShapeDtypeStruct((2 * LANES // SUB, SUB * span // LANES, LANES), jnp.float32),
        scratch_shapes=[
            pltpu.VMEM((2 * span, LANES), jnp.float32),
            pltpu.VMEM((span, 2 * LANES), jnp.float32),
        ],
        compiler_params=pltpu.CompilerParams(vmem_limit_bytes=48 << 20),
    )(mid, turn, fh, fl, arrived), kept


def order_kernel(sources, in_ref, out_ref, whole):
    count = len(sources)
    fold = LANES // count
    each = in_ref.shape[0] // count
    tiles = each // SUB // fold
    lows = SUB // 2
    for k, at in enumerate(sources):
        whole[k * each : (k + 1) * each, :] = in_ref[at * each : (at + 1) * each, :]
    for c in range(2):
        for low in range(lows):
            for t in range(tiles):
                parts = [
                    whole[pl.ds((v * tiles + t) * SUB + c * lows + low, count, each), :] for v in range(fold)
                ]
                base = (low * tiles + t) * LANES * 2 + c
                out_ref[pl.ds(base, LANES, 2), :] = jnp.concatenate(parts, 0).T


def order_rows(landed, sources):
    return pl.pallas_call(
        functools.partial(order_kernel, sources),
        out_shape=jax.ShapeDtypeStruct(landed.shape, jnp.float32),
        scratch_shapes=[pltpu.VMEM(landed.shape, jnp.float32)],
        compiler_params=pltpu.CompilerParams(vmem_limit_bytes=32 << 20),
    )(landed)


VMEM_WHOLE = pl.BlockSpec(memory_space=pltpu.VMEM)
FAR_FIRST = (0, 2, 3, 1)


def own_place():
    return lax.axis_index("grp") * 8 + lax.axis_index("dev")


def spread(row, at):
    return jnp.broadcast_to(row[:, at : at + 1], (SUB, LANES))


def mix_kernel(woven, coef_ref, *refs):
    ins, outs = [None] * 4, [None] * 4
    for n, m in enumerate(FAR_FIRST):
        ins[m], outs[m] = refs[n], refs[4 + n]
    rows = refs[0].shape[0] // 2
    row = coef_ref[pl.ds(own_place(), 1), :]
    parity = spread(row, 0)
    turns = [(spread(row, 1 + 2 * m), spread(row, 2 + 2 * m)) for m in range(2)]
    blocks = len(woven)
    for b in range(blocks):
        factors = [(spread(row, 5 + 8 * b + 2 * m), spread(row, 6 + 8 * b + 2 * m)) for m in range(4)]
        for r in range(b * rows // blocks, (b + 1) * rows // blocks, SUB):
            if woven[b]:
                values = [(ref[pl.ds(2 * r, SUB, 2), :], ref[pl.ds(2 * r + 1, SUB, 2), :]) for ref in ins]
            else:
                values = [(ref[r : r + SUB, :], ref[rows + r : rows + r + SUB, :]) for ref in ins]
            (r0, i0), (r1, i1), (r2, i2), (r3, i3) = values
            r2, i2, r3, i3 = r2 * parity, i2 * parity, r3 * parity, i3 * parity
            results = [None] * 4
            for m, (pr, pi, qr, qi) in enumerate(
                ((r0 + r2, i0 + i2, r1 + r3, i1 + i3), (r0 - r2, i0 - i2, r1 - r3, i1 - i3))
            ):
                tc, ts = turns[m]
                tr, ti = qr * tc - qi * ts, qr * ts + qi * tc
                results[m], results[m + 2] = (pr + tr, pi + ti), (pr - tr, pi - ti)
            for out, (re, im), (c, s) in zip(outs, results, factors):
                out[r : r + SUB, :] = re * c - im * s
                out[rows + r : rows + r + SUB, :] = re * s + im * c


def mix(parts, woven, table):
    work = sum(part.size for part in parts)
    mixed = pl.pallas_call(
        functools.partial(mix_kernel, woven),
        in_specs=[VMEM_WHOLE] * 5,
        out_shape=[jax.ShapeDtypeStruct(parts[0].shape, jnp.float32)] * 4,
        cost_estimate=pl.CostEstimate(flops=8 * work, bytes_accessed=8 * work, transcendentals=0),
        compiler_params=pltpu.CompilerParams(vmem_limit_bytes=16 << 20),
    )(table, *[parts[m] for m in FAR_FIRST])
    return [mixed[FAR_FIRST.index(m)] for m in range(4)]


def quarter_kernel(start, in_ref, *refs):
    out_refs, sems = refs[:-1], refs[-1]
    quarter = in_ref.shape[1] // len(out_refs)
    group = lax.axis_index("grp")
    copies = []
    for m, out_ref in enumerate(out_refs):
        at = pl.multiple_of((group ^ m) * quarter + start, LANES)
        copies.append(pltpu.make_async_copy(in_ref.at[:, pl.ds(at, out_ref.shape[1])], out_ref, sems.at[m]))
        copies[-1].start()
    for copy in copies:
        copy.wait()


def quarters(series, start, size):
    parts = pl.pallas_call(
        functools.partial(quarter_kernel, start),
        in_specs=[pl.BlockSpec(memory_space=pl.ANY)],
        out_specs=[VMEM_WHOLE] * 4,
        out_shape=[jax.ShapeDtypeStruct((2, size), jnp.float32)] * 4,
        scratch_shapes=[pltpu.SemaphoreType.DMA((4,))],
        compiler_params=pltpu.CompilerParams(vmem_limit_bytes=56 << 20),
    )(series)
    return [part.reshape(2, size // LANES, LANES).transpose(1, 0, 2).reshape(-1, LANES) for part in parts]


def swap(parts, shift):
    return [send(part, m << shift) if m else part for m, part in enumerate(parts)]


def send(part, flip):
    return lax.ppermute(part, AXES, [(d, d ^ flip) for d in range(lax.axis_size(AXES))])


def device_digits():
    d = np.arange(32)
    z, yx, core = d // 8, d // 2 % 4, d % 2
    return z, yx, core, yx + 4 * z + 16 * core


def root(product, modulus):
    c, s = roots(product, modulus)
    return c + 1j * s


def rows_of(columns):
    flat = [columns[0].real] + [part for column in columns[1:] for part in (column.real, column.imag)]
    table = np.zeros((32, LANES), np.float32)
    table[:, : len(flat)] = np.stack(flat, 1)
    return table


def mix_table(mine, digit, factors):
    columns = [root((mine ^ 2) * digit - mine * digit, 4)]
    columns += [root(((mine ^ 1) - mine) * (digit ^ m), 4) for m in range(2)]
    return rows_of(columns + [f * root(mine * (digit ^ m), 4) for block in factors for m, f in enumerate(block)])


def mix_tables(points, start, rows):
    z, yx, core, _ = device_digits()
    first = [[root((2 * yx + core) * (yx ^ m), 32) / math.sqrt(points) for m in range(4)]]
    second = [
        [root(core * (z ^ m), 8) * root((yx + 4 * (z ^ m)) * (z * 8 + start // 32 + b), 1024) for m in range(4)]
        for b in range(rows // 32)
    ]
    return mix_table(z, yx, first), mix_table(yx, z, second)


def slab_kernel(starts, bit_ref, near_ref, mid_ref, turn_ref, fh_ref, fl_ref, *refs):
    in_refs, (out_ref, whole, first, second) = refs[:-4], refs[-4:]
    place = own_place()
    group, pair, core = place // 8, place // 2 % 4, place % 2
    digit = pair + 4 * group + 16 * core
    row = bit_ref[pl.ds(place, 1), :]
    sign = spread(row, 0)
    span, block = 1024, 0
    for h, start in enumerate(starts):
        for m in range(4):
            mine, other = in_refs[h * 8 + FAR_FIRST.index(m)], in_refs[h * 8 + 4 + FAR_FIRST.index(m)]
            rows = mine.shape[0] // 2
            at = pl.multiple_of((group ^ m) * (span // 4) + start, 32)
            for b in range(0, rows, 32):
                c, s = spread(row, 1 + 2 * block), spread(row, 2 + 2 * block)
                block += 1
                for r in range(b, b + 32, SUB):
                    re = other[r : r + SUB, :] + mine[r : r + SUB, :] * sign
                    im = other[rows + r : rows + r + SUB, :] + mine[rows + r : rows + r + SUB, :] * sign
                    whole[pl.ds(at + r, SUB), :] = re * c - im * s
                    whole[pl.ds(span + at + r, SUB), :] = re * s + im * c
    outer = inner = 32
    for j in range(0, inner, SUB):
        values = []
        for e in range(outer):
            base = e * inner + j
            values.append((whole[base : base + SUB, :], whole[span + base : span + base + SUB, :]))
        at = pl.multiple_of(digit * 2 * inner + j, SUB)
        nc, ns = near_ref[pl.ds(at, SUB), :], near_ref[pl.ds(at + inner, SUB), :]
        for k, (re, im) in enumerate(dft_list(values)):
            base = k * inner + j
            mc, ms = mid_ref[base : base + SUB, :], mid_ref[span + base : span + base + SUB, :]
            c, s = mc * nc - ms * ns, mc * ns + ms * nc
            first[base : base + SUB, :] = re * c - im * s
            first[span + base : span + base + SUB, :] = re * s + im * c
    lane_stage(outer, inner, turn_ref, fh_ref, fl_ref, out_ref, first, second)


def slab_transform(arrived, lane_rows, points):
    z, _, core, _ = device_digits()
    nc, ns = roots(np.arange(32)[:, None] * np.arange(32 * LANES)[None, :], points)
    near = np.stack([nc, ns], 1).reshape(32 * 2 * 32, LANES).astype(np.float32)
    mid, turn, fh, fl, _ = local_tables(32, 32, lane_rows)
    starts = [sum(CHUNKS[:h]) for h in range(len(CHUNKS))]
    bits = [1 - 2 * core + 0j]
    for start, rows in zip(starts, CHUNKS):
        for m in range(4):
            bits += [root(core * ((z ^ m) * 8 + start // 32 + b), 64) for b in range(rows // 32)]
    return pl.pallas_call(
        functools.partial(slab_kernel, starts),
        in_specs=[VMEM_WHOLE] * (6 + len(arrived)),
        out_shape=jax.ShapeDtypeStruct((32, 64, LANES), jnp.float32),
        scratch_shapes=[
            pltpu.VMEM((2048, LANES), jnp.float32),
            pltpu.VMEM((2048, LANES), jnp.float32),
            pltpu.VMEM((1024, 2 * LANES), jnp.float32),
        ],
        compiler_params=pltpu.CompilerParams(vmem_limit_bytes=48 << 20),
    )(rows_of(bits), near, mid, turn, fh, fl, *arrived)


CHUNKS = (128, 128)


def by_axes(series, points):
    slab = series.shape[1]
    arrived = []
    for h, rows in enumerate(CHUNKS):
        start = sum(CHUNKS[:h])
        first, second = mix_tables(points, start, rows)
        parts = swap(quarters(series, start * LANES, rows * LANES), 3)
        parts = swap(mix(parts, (True,), first), 1)
        parts = swap(mix(parts, (False,) * (rows // 32), second), 3)
        mine = [parts[m] for m in FAR_FIRST]
        arrived += mine + [send(part, 1) for part in mine]
    dest, c, low = np.meshgrid(np.arange(32), np.arange(2), np.arange(4), indexing="ij")
    lane_rows = ((dest * 4 + low).reshape(-1), (c == 1).reshape(-1))
    spectrum = slab_transform(arrived, lane_rows, points)
    landed = lax.all_to_all(spectrum, AXES, split_axis=0, concat_axis=0, tiled=True).reshape(2048, LANES)
    ordered = order_rows(landed, np.argsort(device_digits()[3]).tolist())
    return ordered.reshape(slab // LANES, 2, LANES).transpose(1, 0, 2).reshape(2, slab)


def exchange(blocks, count):
    shape = blocks.shape
    blocks = blocks.reshape((count, shape[0] // count) + shape[1:])
    return lax.all_to_all(blocks, ORDER, split_axis=0, concat_axis=0, tiled=True).reshape(shape)


def local(series):
    count = lax.axis_size("grp") * lax.axis_size("dev")
    slab = series.shape[1]
    points = slab * count
    piece_rows = slab // count // LANES
    if (lax.axis_size("grp"), lax.axis_size("dev"), slab) == (4, 8, 1024 * LANES):
        return by_axes(series, points)
    at = np.arange(count).reshape(lax.axis_size("dev"), lax.axis_size("grp")).T.reshape(-1)
    owners = np.argsort(at)
    tiles = series.reshape(2, count, piece_rows, LANES).transpose(1, 2, 0, 3)
    received = exchange(tiles, count).reshape(2 * slab // LANES, LANES)
    turned = across(received, at.tolist(), points, 1.0 / math.sqrt(points))
    arrived = exchange(turned, count)
    if 2 * LANES == SUB * count:
        lows = LANES // count
        dest, c, low = np.meshgrid(owners, np.arange(2), np.arange(lows), indexing="ij")
        lane_rows = ((dest * lows + low).reshape(-1), (c == 1).reshape(-1))
        spectrum, _ = local_transform(arrived, count, piece_rows, lane_rows)
        landed = exchange(spectrum.reshape(turned.shape), count)
        ordered = order_rows(landed, list(range(count)))
        return ordered.reshape(slab // LANES, 2, LANES).transpose(1, 0, 2).reshape(2, slab)
    freq, c = np.meshgrid(np.arange(LANES), np.arange(2), indexing="ij")
    spectrum, kept = local_transform(arrived, count, piece_rows, (freq.reshape(-1), (c == 1).reshape(-1)))
    spectrum = spectrum.reshape(2 * LANES // SUB, -1, SUB, LANES).transpose(0, 2, 1, 3).reshape(2 * LANES, -1)
    natural = jnp.take(spectrum, np.argsort(kept), axis=1).reshape(LANES, 2, -1)
    blocks = natural.transpose(0, 2, 1).reshape(count, -1, 2)[owners]
    landed = exchange(blocks, count)
    return landed.transpose(2, 1, 0).reshape(2, slab)


def solution(mesh):
    return jax.shard_map(
        local,
        mesh=mesh,
        in_specs=(P(None, AXES),),
        out_specs=P(None, AXES),
        check_vma=False,
    )
```

profile of v0, /device:TPU:0, one launch (start us, length us, event | category | flops | bytes accessed | tf_op | source)
XLA Modules:
  0.0 96.9 jit_solution(7783018908652435750)
XLA Ops:
  0.0 2.0 %shard_map.112 = (f32[2,16384]{1,0:T(2,128)}, f32[2,16384]{1,0:T(2,128)}, f32[2,16384]{1,0:T(2,128)}, f32[2,16384]{1,0:T(2,128)}) custom-call(f32[2,131072]{1,0:T(2,128)} %in_ref.3), custom_call_target="tpu_custom_call" | custom-call | tf_op jit(solution)/shard_map/pallas_call | solution.py:282
  2.0 4.1 %collective-permute-start.13 = (f32[256,128]{1,0:T(8,128)}, f32[256,128]{1,0:T(8,128)S(1)}, u32[]{:S(2)}, u32[]{:S(2)}) collective-permute-start(f32[256,128]{1,0:T(8,128)} %bitcast.54), channel_id=1, source_target_pairs={{0,16},{1,17},{2,18},{3,19},{4,20},{5,21},{6,22},{7,23},{8,24},{9,... | collective-permute-start | bytes 393224 | tf_op jit(solution)/shard_map/ppermute | solution.py:298
  6.1 1.3 %collective-permute-start.14 = (f32[256,128]{1,0:T(8,128)}, f32[256,128]{1,0:T(8,128)S(1)}, u32[]{:S(2)}, u32[]{:S(2)}) collective-permute-start(f32[256,128]{1,0:T(8,128)} %bitcast.53), channel_id=1, source_target_pairs={{0,24},{1,25},{2,26},{3,27},{4,28},{5,29},{6,30},{7,31},{8,16},{9,... | collective-permute-start | bytes 393224 | tf_op jit(solution)/shard_map/ppermute | solution.py:298
  7.7 2.0 %shard_map.109 = (f32[2,16384]{1,0:T(2,128)}, f32[2,16384]{1,0:T(2,128)}, f32[2,16384]{1,0:T(2,128)}, f32[2,16384]{1,0:T(2,128)}) custom-call(f32[2,131072]{1,0:T(2,128)} %in_ref.3), custom_call_target="tpu_custom_call" | custom-call | tf_op jit(solution)/shard_map/pallas_call | solution.py:282
  9.7 2.9 %collective-permute-start = (f32[256,128]{1,0:T(8,128)}, f32[256,128]{1,0:T(8,128)S(1)}, u32[]{:S(2)}, u32[]{:S(2)}) collective-permute-start(f32[256,128]{1,0:T(8,128)} %bitcast.51), channel_id=1, source_target_pairs={{0,16},{1,17},{2,18},{3,19},{4,20},{5,21},{6,22},{7,23},{8,24},{9,... | collective-permute-start | bytes 393224 | tf_op jit(solution)/shard_map/ppermute | solution.py:298
  12.5 1.3 %collective-permute-start.1 = (f32[256,128]{1,0:T(8,128)}, f32[256,128]{1,0:T(8,128)S(1)}, u32[]{:S(2)}, u32[]{:S(2)}) collective-permute-start(f32[256,128]{1,0:T(8,128)} %bitcast.50), channel_id=1, source_target_pairs={{0,24},{1,25},{2,26},{3,27},{4,28},{5,29},{6,30},{7,31},{8,16},{9,... | collective-permute-start | bytes 393224 | tf_op jit(solution)/shard_map/ppermute | solution.py:298
  13.9 2.9 %collective-permute-done.13.refs_1_ = f32[256,128]{1,0:T(8,128)S(1)} collective-permute-done((f32[256,128]{1,0:T(8,128)}, f32[256,128]{1,0:T(8,128)S(1)}, u32[]{:S(2)}, u32[]{:S(2)}) %collective-permute-start.13) | collective-permute-done | bytes 131104 | tf_op jit(solution)/shard_map/ppermute | solution.py:298
  17.6 5.8 %collective-permute-start.16 = (f32[256,128]{1,0:T(8,128)S(1)}, f32[256,128]{1,0:T(8,128)S(1)}, u32[]{:S(2)}, u32[]{:S(2)}) collective-permute-start(f32[256,128]{1,0:T(8,128)S(1)} %get-tuple-element.46), channel_id=1, source_target_pairs={{0,4},{1,5},{2,6},{3,7},{4,0},{5,1},{6,2},{7,3},{8,12},{9,13},{10,... | collective-permute-start | bytes 393224 | tf_op jit(solution)/shard_map/ppermute | solution.py:298
  23.4 1.4 %collective-permute-start.17 = (f32[256,128]{1,0:T(8,128)S(1)}, f32[256,128]{1,0:T(8,128)S(1)}, u32[]{:S(2)}, u32[]{:S(2)}) collective-permute-start(f32[256,128]{1,0:T(8,128)S(1)} %get-tuple-element.47), channel_id=1, source_target_pairs={{0,6},{1,7},{2,4},{3,5},{4,2},{5,3},{6,0},{7,1},{8,14},{9,15},{10,... | collective-permute-start | bytes 393224 | tf_op jit(solution)/shard_map/ppermute | solution.py:298
  24.8 2.7 %collective-permute-done.refs_1_ = f32[256,128]{1,0:T(8,128)S(1)} collective-permute-done((f32[256,128]{1,0:T(8,128)}, f32[256,128]{1,0:T(8,128)S(1)}, u32[]{:S(2)}, u32[]{:S(2)}) %collective-permute-start) | collective-permute-done | bytes 131104 | tf_op jit(solution)/shard_map/ppermute | solution.py:298
  27.5 1.8 %collective-permute-start.18 = (f32[256,128]{1,0:T(8,128)S(1)}, f32[256,128]{1,0:T(8,128)S(1)}, u32[]{:S(2)}, u32[]{:S(2)}) collective-permute-start(f32[256,128]{1,0:T(8,128)S(1)} %get-tuple-element.48), channel_id=1, source_target_pairs={{0,2},{1,3},{2,0},{3,1},{4,6},{5,7},{6,4},{7,5},{8,10},{9,11},{10,... | collective-permute-start | bytes 393224 | tf_op jit(solution)/shard_map/ppermute | solution.py:298
  29.3 0.9 copy-done.4
  30.5 1.6 %collective-permute-start.3 = (f32[256,128]{1,0:T(8,128)S(1)}, f32[256,128]{1,0:T(8,128)S(1)}, u32[]{:S(2)}, u32[]{:S(2)}) collective-permute-start(f32[256,128]{1,0:T(8,128)S(1)} %get-tuple-element.34), channel_id=1, source_target_pairs={{0,4},{1,5},{2,6},{3,7},{4,0},{5,1},{6,2},{7,3},{8,12},{9,13},{10,... | collective-permute-start | bytes 393224 | tf_op jit(solution)/shard_map/ppermute | solution.py:298
  32.3 1.8 %collective-permute-start.5 = (f32[256,128]{1,0:T(8,128)S(1)}, f32[256,128]{1,0:T(8,128)S(1)}, u32[]{:S(2)}, u32[]{:S(2)}) collective-permute-start(f32[256,128]{1,0:T(8,128)S(1)} %get-tuple-element.36), channel_id=1, source_target_pairs={{0,2},{1,3},{2,0},{3,1},{4,6},{5,7},{6,4},{7,5},{8,10},{9,11},{10,... | collective-permute-start | bytes 393224 | tf_op jit(solution)/shard_map/ppermute | solution.py:298
  34.3 2.8 %collective-permute-start.19 = (f32[256,128]{1,0:T(8,128)S(1)}, f32[256,128]{1,0:T(8,128)S(1)}, u32[]{:S(2)}, u32[]{:S(2)}) collective-permute-start(f32[256,128]{1,0:T(8,128)S(1)} %get-tuple-element.50), channel_id=1, source_target_pairs={{0,16},{1,17},{2,18},{3,19},{4,20},{5,21},{6,22},{7,23},{8,24},{9,... | collective-permute-start | bytes 393224 | tf_op jit(solution)/shard_map/ppermute | solution.py:298
  37.7 1.5 %collective-permute-start.21 = (f32[256,128]{1,0:T(8,128)S(1)}, f32[256,128]{1,0:T(8,128)S(1)}, u32[]{:S(2)}, u32[]{:S(2)}) collective-permute-start(f32[256,128]{1,0:T(8,128)S(1)} %get-tuple-element.52), channel_id=1, source_target_pairs={{0,8},{1,9},{2,10},{3,11},{4,12},{5,13},{6,14},{7,15},{8,0},{9,1},... | collective-permute-start | bytes 393224 | tf_op jit(solution)/shard_map/ppermute | solution.py:298
  39.4 3.7 %collective-permute-start.6 = (f32[256,128]{1,0:T(8,128)S(1)}, f32[256,128]{1,0:T(8,128)S(1)}, u32[]{:S(2)}, u32[]{:S(2)}) collective-permute-start(f32[256,128]{1,0:T(8,128)S(1)} %get-tuple-element.38), channel_id=1, source_target_pairs={{0,16},{1,17},{2,18},{3,19},{4,20},{5,21},{6,22},{7,23},{8,24},{9,... | collective-permute-start | bytes 393224 | tf_op jit(solution)/shard_map/ppermute | solution.py:298
  43.1 4.4 %collective-permute-done.19.refs_9_ = f32[256,128]{1,0:T(8,128)S(1)} collective-permute-done((f32[256,128]{1,0:T(8,128)S(1)}, f32[256,128]{1,0:T(8,128)S(1)}, u32[]{:S(2)}, u32[]{:S(2)}) %collective-permute-start.19) | collective-permute-done | bytes 131104 | tf_op jit(solution)/shard_map/ppermute | solution.py:298
  47.5 6.1 %collective-permute-start.7 = (f32[256,128]{1,0:T(8,128)S(1)}, f32[256,128]{1,0:T(8,128)S(1)}, u32[]{:S(2)}, u32[]{:S(2)}) collective-permute-start(f32[256,128]{1,0:T(8,128)S(1)} %get-tuple-element.39), channel_id=1, source_target_pairs={{0,24},{1,25},{2,26},{3,27},{4,28},{5,29},{6,30},{7,31},{8,16},{9,... | collective-permute-start | bytes 393224 | tf_op jit(solution)/shard_map/ppermute | solution.py:298
  54.2 3.1 %collective-permute-done.6.refs_1_ = f32[256,128]{1,0:T(8,128)S(1)} collective-permute-done((f32[256,128]{1,0:T(8,128)S(1)}, f32[256,128]{1,0:T(8,128)S(1)}, u32[]{:S(2)}, u32[]{:S(2)}) %collective-permute-start.6) | collective-permute-done | bytes 131104 | tf_op jit(solution)/shard_map/ppermute | solution.py:298
  57.8 1.9 %collective-permute-done.8.refs_3_ = f32[256,128]{1,0:T(8,128)S(1)} collective-permute-done((f32[256,128]{1,0:T(8,128)S(1)}, f32[256,128]{1,0:T(8,128)S(1)}, u32[]{:S(2)}, u32[]{:S(2)}) %collective-permute-start.8) | collective-permute-done | bytes 131104 | tf_op jit(solution)/shard_map/ppermute | solution.py:298
  61.6 3.6 %shard_map.115 = f32[32,64,128]{2,1,0:T(8,128)S(1)} custom-call(f32[32,128]{1,0:T(8,128)S(1)} %copy-done.7, f32[2048,128]{1,0:T(8,128)S(1)} %copy-done.1, f32[2048,128]{1,0:T(8,128)S(1)} %copy-done, f32[2048,128]{1,0:T(8,128)} %constant.24.clone.turn_ref, bf16[256,256]{1,0:T(8,128)(2,1)S(1)} %copy-done.3, bf16[256,256]{1,0:T(8,128)(2,1)S(1)} %copy-done.2, ...), custom_call_target="tpu_custom_call" | custom-call | tf_op jit(solution)/shard_map/pallas_call | solution.py:383
  65.2 29.9 %all_to_all.5 = f32[32,64,128]{2,1,0:T(8,128)S(1)} all-to-all(f32[32,64,128]{2,1,0:T(8,128)S(1)} %shard_map.115), channel_id=1, replica_groups=mesh['grp'=4,'dev'=8] {'grp','dev'}, dimensions={0} | all-to-all | bytes 2097152 | tf_op jit(solution)/shard_map/all_to_all | solution.py:413
  95.1 1.8 %shard_map.116 = f32[2048,128]{1,0:T(8,128)} custom-call(f32[2048,128]{1,0:T(8,128)S(1)} %bitcast.46), custom_call_target="tpu_custom_call" | custom-call | tf_op jit(solution)/shard_map/pallas_call | solution.py:206
  (57 shorter events, 5.4 us)
Async XLA Ops:
  2.0 14.9 %collective-permute-start.13 = (f32[256,128]{1,0:T(8,128)}, f32[256,128]{1,0:T(8,128)S(1)}, u32[]{:S(2)}, u32[]{:S(2)}) collective-permute-start(f32[256,128]{1,0:T(8,128)} %bitcast.54), channel_id=1, source_target_pairs={{0,16},{1,17},{2,18},{3,19},{4,20},{5,21},{6,22},{7,23},{8,24},{9,... | collective-permute-start | bytes 393224 | tf_op jit(solution)/shard_map/ppermute | solution.py:298
  6.1 11.2 %collective-permute-start.14 = (f32[256,128]{1,0:T(8,128)}, f32[256,128]{1,0:T(8,128)S(1)}, u32[]{:S(2)}, u32[]{:S(2)}) collective-permute-start(f32[256,128]{1,0:T(8,128)} %bitcast.53), channel_id=1, source_target_pairs={{0,24},{1,25},{2,26},{3,27},{4,28},{5,29},{6,30},{7,31},{8,16},{9,... | collective-permute-start | bytes 393224 | tf_op jit(solution)/shard_map/ppermute | solution.py:298
  7.4 9.9 %collective-permute-start.15 = (f32[256,128]{1,0:T(8,128)}, f32[256,128]{1,0:T(8,128)S(1)}, u32[]{:S(2)}, u32[]{:S(2)}) collective-permute-start(f32[256,128]{1,0:T(8,128)} %bitcast.52), channel_id=1, source_target_pairs={{0,8},{1,9},{2,10},{3,11},{4,12},{5,13},{6,14},{7,15},{8,0},{9,1},... | collective-permute-start | bytes 393224 | tf_op jit(solution)/shard_map/ppermute | solution.py:298
  9.7 17.8 %collective-permute-start = (f32[256,128]{1,0:T(8,128)}, f32[256,128]{1,0:T(8,128)S(1)}, u32[]{:S(2)}, u32[]{:S(2)}) collective-permute-start(f32[256,128]{1,0:T(8,128)} %bitcast.51), channel_id=1, source_target_pairs={{0,16},{1,17},{2,18},{3,19},{4,20},{5,21},{6,22},{7,23},{8,24},{9,... | collective-permute-start | bytes 393224 | tf_op jit(solution)/shard_map/ppermute | solution.py:298
  12.5 16.8 %collective-permute-start.1 = (f32[256,128]{1,0:T(8,128)}, f32[256,128]{1,0:T(8,128)S(1)}, u32[]{:S(2)}, u32[]{:S(2)}) collective-permute-start(f32[256,128]{1,0:T(8,128)} %bitcast.50), channel_id=1, source_target_pairs={{0,24},{1,25},{2,26},{3,27},{4,28},{5,29},{6,30},{7,31},{8,16},{9,... | collective-permute-start | bytes 393224 | tf_op jit(solution)/shard_map/ppermute | solution.py:298
  16.8 12.5 %collective-permute-start.2 = (f32[256,128]{1,0:T(8,128)}, f32[256,128]{1,0:T(8,128)S(1)}, u32[]{:S(2)}, u32[]{:S(2)}) collective-permute-start(f32[256,128]{1,0:T(8,128)} %bitcast.49), channel_id=1, source_target_pairs={{0,8},{1,9},{2,10},{3,11},{4,12},{5,13},{6,14},{7,15},{8,0},{9,1},... | collective-permute-start | bytes 393224 | tf_op jit(solution)/shard_map/ppermute | solution.py:298
  17.6 14.7 %collective-permute-start.16 = (f32[256,128]{1,0:T(8,128)S(1)}, f32[256,128]{1,0:T(8,128)S(1)}, u32[]{:S(2)}, u32[]{:S(2)}) collective-permute-start(f32[256,128]{1,0:T(8,128)S(1)} %get-tuple-element.46), channel_id=1, source_target_pairs={{0,4},{1,5},{2,6},{3,7},{4,0},{5,1},{6,2},{7,3},{8,12},{9,13},{10,... | collective-permute-start | bytes 393224 | tf_op jit(solution)/shard_map/ppermute | solution.py:298
  23.4 10.7 %collective-permute-start.17 = (f32[256,128]{1,0:T(8,128)S(1)}, f32[256,128]{1,0:T(8,128)S(1)}, u32[]{:S(2)}, u32[]{:S(2)}) collective-permute-start(f32[256,128]{1,0:T(8,128)S(1)} %get-tuple-element.47), channel_id=1, source_target_pairs={{0,6},{1,7},{2,4},{3,5},{4,2},{5,3},{6,0},{7,1},{8,14},{9,15},{10,... | collective-permute-start | bytes 393224 | tf_op jit(solution)/shard_map/ppermute | solution.py:298
  27.5 6.6 %collective-permute-start.18 = (f32[256,128]{1,0:T(8,128)S(1)}, f32[256,128]{1,0:T(8,128)S(1)}, u32[]{:S(2)}, u32[]{:S(2)}) collective-permute-start(f32[256,128]{1,0:T(8,128)S(1)} %get-tuple-element.48), channel_id=1, source_target_pairs={{0,2},{1,3},{2,0},{3,1},{4,6},{5,7},{6,4},{7,5},{8,10},{9,11},{10,... | collective-permute-start | bytes 393224 | tf_op jit(solution)/shard_map/ppermute | solution.py:298
  30.5 7.2 %collective-permute-start.3 = (f32[256,128]{1,0:T(8,128)S(1)}, f32[256,128]{1,0:T(8,128)S(1)}, u32[]{:S(2)}, u32[]{:S(2)}) collective-permute-start(f32[256,128]{1,0:T(8,128)S(1)} %get-tuple-element.34), channel_id=1, source_target_pairs={{0,4},{1,5},{2,6},{3,7},{4,0},{5,1},{6,2},{7,3},{8,12},{9,13},{10,... | collective-permute-start | bytes 393224 | tf_op jit(solution)/shard_map/ppermute | solution.py:298
  32.1 7.1 %collective-permute-start.4 = (f32[256,128]{1,0:T(8,128)S(1)}, f32[256,128]{1,0:T(8,128)S(1)}, u32[]{:S(2)}, u32[]{:S(2)}) collective-permute-start(f32[256,128]{1,0:T(8,128)S(1)} %get-tuple-element.35), channel_id=1, source_target_pairs={{0,6},{1,7},{2,4},{3,5},{4,2},{5,3},{6,0},{7,1},{8,14},{9,15},{10,... | collective-permute-start | bytes 393224 | tf_op jit(solution)/shard_map/ppermute | solution.py:298
  32.3 6.9 %collective-permute-start.5 = (f32[256,128]{1,0:T(8,128)S(1)}, f32[256,128]{1,0:T(8,128)S(1)}, u32[]{:S(2)}, u32[]{:S(2)}) collective-permute-start(f32[256,128]{1,0:T(8,128)S(1)} %get-tuple-element.36), channel_id=1, source_target_pairs={{0,2},{1,3},{2,0},{3,1},{4,6},{5,7},{6,4},{7,5},{8,10},{9,11},{10,... | collective-permute-start | bytes 393224 | tf_op jit(solution)/shard_map/ppermute | solution.py:298
  34.3 13.2 %collective-permute-start.19 = (f32[256,128]{1,0:T(8,128)S(1)}, f32[256,128]{1,0:T(8,128)S(1)}, u32[]{:S(2)}, u32[]{:S(2)}) collective-permute-start(f32[256,128]{1,0:T(8,128)S(1)} %get-tuple-element.50), channel_id=1, source_target_pairs={{0,16},{1,17},{2,18},{3,19},{4,20},{5,21},{6,22},{7,23},{8,24},{9,... | collective-permute-start | bytes 393224 | tf_op jit(solution)/shard_map/ppermute | solution.py:298
  37.1 16.4 %collective-permute-start.20 = (f32[256,128]{1,0:T(8,128)S(1)}, f32[256,128]{1,0:T(8,128)S(1)}, u32[]{:S(2)}, u32[]{:S(2)}) collective-permute-start(f32[256,128]{1,0:T(8,128)S(1)} %get-tuple-element.51), channel_id=1, source_target_pairs={{0,24},{1,25},{2,26},{3,27},{4,28},{5,29},{6,30},{7,31},{8,16},{9,... | collective-permute-start | bytes 393224 | tf_op jit(solution)/shard_map/ppermute | solution.py:298
  37.7 16.0 %collective-permute-start.21 = (f32[256,128]{1,0:T(8,128)S(1)}, f32[256,128]{1,0:T(8,128)S(1)}, u32[]{:S(2)}, u32[]{:S(2)}) collective-permute-start(f32[256,128]{1,0:T(8,128)S(1)} %get-tuple-element.52), channel_id=1, source_target_pairs={{0,8},{1,9},{2,10},{3,11},{4,12},{5,13},{6,14},{7,15},{8,0},{9,1},... | collective-permute-start | bytes 393224 | tf_op jit(solution)/shard_map/ppermute | solution.py:298
  39.2 14.5 %collective-permute-start.22 = (f32[256,128]{1,0:T(8,128)S(1)}, f32[256,128]{1,0:T(8,128)S(1)}, u32[]{:S(2)}, u32[]{:S(2)}) collective-permute-start(f32[256,128]{1,0:T(8,128)S(1)} %get-tuple-element.49.refs_8_), channel_id=1, source_target_pairs={{0,1},{1,0},{2,3},{3,2},{4,5},{5,4},{6,7},{7,6},{8,9},{9,8},{10,11... | collective-permute-start | bytes 393224 | tf_op jit(solution)/shard_map/ppermute | solution.py:298
  39.4 17.9 %collective-permute-start.6 = (f32[256,128]{1,0:T(8,128)S(1)}, f32[256,128]{1,0:T(8,128)S(1)}, u32[]{:S(2)}, u32[]{:S(2)}) collective-permute-start(f32[256,128]{1,0:T(8,128)S(1)} %get-tuple-element.38), channel_id=1, source_target_pairs={{0,16},{1,17},{2,18},{3,19},{4,20},{5,21},{6,22},{7,23},{8,24},{9,... | collective-permute-start | bytes 393224 | tf_op jit(solution)/shard_map/ppermute | solution.py:298
  47.5 9.8 %collective-permute-start.7 = (f32[256,128]{1,0:T(8,128)S(1)}, f32[256,128]{1,0:T(8,128)S(1)}, u32[]{:S(2)}, u32[]{:S(2)}) collective-permute-start(f32[256,128]{1,0:T(8,128)S(1)} %get-tuple-element.39), channel_id=1, source_target_pairs={{0,24},{1,25},{2,26},{3,27},{4,28},{5,29},{6,30},{7,31},{8,16},{9,... | collective-permute-start | bytes 393224 | tf_op jit(solution)/shard_map/ppermute | solution.py:298
  53.6 6.1 %collective-permute-start.8 = (f32[256,128]{1,0:T(8,128)S(1)}, f32[256,128]{1,0:T(8,128)S(1)}, u32[]{:S(2)}, u32[]{:S(2)}) collective-permute-start(f32[256,128]{1,0:T(8,128)S(1)} %get-tuple-element.40), channel_id=1, source_target_pairs={{0,8},{1,9},{2,10},{3,11},{4,12},{5,13},{6,14},{7,15},{8,0},{9,1},... | collective-permute-start | bytes 393224 | tf_op jit(solution)/shard_map/ppermute | solution.py:298
  53.7 6.0 %collective-permute-start.9 = (f32[256,128]{1,0:T(8,128)S(1)}, f32[256,128]{1,0:T(8,128)S(1)}, u32[]{:S(2)}, u32[]{:S(2)}) collective-permute-start(f32[256,128]{1,0:T(8,128)S(1)} %get-tuple-element.37.refs_0_), channel_id=1, source_target_pairs={{0,1},{1,0},{2,3},{3,2},{4,5},{5,4},{6,7},{7,6},{8,9},{9,8},{10,11... | collective-permute-start | bytes 393224 | tf_op jit(solution)/shard_map/ppermute | solution.py:298
  53.7 6.5 %collective-permute-start.23 = (f32[256,128]{1,0:T(8,128)S(1)}, f32[256,128]{1,0:T(8,128)S(1)}, u32[]{:S(2)}, u32[]{:S(2)}) collective-permute-start(f32[256,128]{1,0:T(8,128)S(1)} %collective-permute-done.19.refs_9_), channel_id=1, source_target_pairs={{0,1},{1,0},{2,3},{3,2},{4,5},{5,4},{6,7},{7,6},{8,9},{9,8},{10,11... | collective-permute-start | bytes 393224 | tf_op jit(solution)/shard_map/ppermute | solution.py:298
  57.3 3.0 %collective-permute-start.24 = (f32[256,128]{1,0:T(8,128)S(1)}, f32[256,128]{1,0:T(8,128)S(1)}, u32[]{:S(2)}, u32[]{:S(2)}) collective-permute-start(f32[256,128]{1,0:T(8,128)S(1)} %collective-permute-done.20.refs_10_), channel_id=1, source_target_pairs={{0,1},{1,0},{2,3},{3,2},{4,5},{5,4},{6,7},{7,6},{8,9},{9,8},{10,11... | collective-permute-start | bytes 393224 | tf_op jit(solution)/shard_map/ppermute | solution.py:298
  57.3 3.0 %collective-permute-start.25 = (f32[256,128]{1,0:T(8,128)S(1)}, f32[256,128]{1,0:T(8,128)S(1)}, u32[]{:S(2)}, u32[]{:S(2)}) collective-permute-start(f32[256,128]{1,0:T(8,128)S(1)} %collective-permute-done.21.refs_11_), channel_id=1, source_target_pairs={{0,1},{1,0},{2,3},{3,2},{4,5},{5,4},{6,7},{7,6},{8,9},{9,8},{10,11... | collective-permute-start | bytes 393224 | tf_op jit(solution)/shard_map/ppermute | solution.py:298
  59.7 1.5 %collective-permute-start.11 = (f32[256,128]{1,0:T(8,128)S(1)}, f32[256,128]{1,0:T(8,128)S(1)}, u32[]{:S(2)}, u32[]{:S(2)}) collective-permute-start(f32[256,128]{1,0:T(8,128)S(1)} %collective-permute-done.7.refs_2_), channel_id=1, source_target_pairs={{0,1},{1,0},{2,3},{3,2},{4,5},{5,4},{6,7},{7,6},{8,9},{9,8},{10,11... | collective-permute-start | bytes 393224 | tf_op jit(solution)/shard_map/ppermute | solution.py:298
  (12 other events, 299.8 us)
where the time goes:
time: 97.1 us; the launch traced here: 96.9 us
  starting transfers between devices  39.3 us (40%)
  blocking collectives  29.9 us (31%)
  waiting for transfers between devices  16.3 us (17%)
  Pallas kernels  10.2 us (11%)
    ppermute x26, starting transfers between devices, send(): lax.ppermute(part, AXES, [(d, d ^ flip) for d in range(lax.axis_size(AXES...  39.3 us
    all_to_all x1, blocking collectives, by_axes(): lax.all_to_all(spectrum, AXES, split_axis=0, concat_axis=0, tiled=True)  29.9 us
    ppermute x26, waiting for transfers between devices, send(): lax.ppermute(part, AXES, [(d, d ^ flip) for d in range(lax.axis_size(AXES...  16.3 us
    pallas_call x2, Pallas kernels, quarters(): pl.pallas_call(functools.partial(quarter_kernel, start), in_specs=[pl.Blo...  3.95 us
    pallas_call x1, Pallas kernels, slab_transform(): pl.pallas_call(functools.partial(slab_kernel, starts), in_specs=[VMEM_WHO...  3.56 us
  transfers between devices with their start and end apart: 26, of which 8 were waited for; matrix products, arithmetic and copies ran while one was open for 0% of the time, Pallas kernels for 3%

commit v1 on v0

--- a/solution.py
+++ b/solution.py
@@ -109,29 +109,34 @@
 def lane_stage(outer, inner, turn_ref, fh_ref, fl_ref, out_ref, first, second):
     span = outer * inner
     fold = outer // SUB
-    for v in range(fold):
-        values = []
-        for j in range(inner):
-            base = v * inner + j
-            values.append(
-                (
-                    first[pl.ds(base, SUB, fold * inner), :],
-                    first[pl.ds(span + base, SUB, fold * inner), :],
-                )
-            )
-        for k, (re, im) in enumerate(dft_list(values)):
-            base = (v * inner + k) * SUB
-            c, s = turn_ref[base : base + SUB, :], turn_ref[span + base : span + base + SUB, :]
-            second[base : base + SUB, :LANES] = re * c - im * s
-            second[base : base + SUB, LANES:] = re * s + im * c
-    xh, xl = split_bf16(second[...])
+    together = max(1, LANES // (inner * SUB))
     dot = functools.partial(
         lax.dot_general, dimension_numbers=(((1,), (1,)), ((), ())), preferred_element_type=jnp.float32
     )
-    result = dot(fh_ref[...], xh) + (dot(fh_ref[...], xl) + dot(fl_ref[...], xh))
-    for t in range(span // LANES):
-        tile = result[:, t * LANES : (t + 1) * LANES]
-        out_ref[:, t * SUB : (t + 1) * SUB, :] = tile.reshape(tile.shape[0] // SUB, SUB, LANES)
+    for begin in range(0, fold, together):
+        for v in range(begin, begin + together):
+            values = []
+            for j in range(inner):
+                base = v * inner + j
+                values.append(
+                    (
+                        first[pl.ds(base, SUB, fold * inner), :],
+                        first[pl.ds(span + base, SUB, fold * inner), :],
+                    )
+                )
+            for k, (re, im) in enumerate(dft_list(values)):
+                base = (v * inner + k) * SUB
+                c, s = turn_ref[base : base + SUB, :], turn_ref[span + base : span + base + SUB, :]
+                second[base : base + SUB, :LANES] = re * c - im * s
+                second[base : base + SUB, LANES:] = re * s + im * c
+        columns = together * inner * SUB
+        done = begin * inner * SUB
+        xh, xl = split_bf16(second[done : done + columns, :])
+        result = dot(fh_ref[...], xh) + (dot(fh_ref[...], xl) + dot(fl_ref[...], xh))
+        for t in range(columns // LANES):
+            tile = result[:, t * LANES : (t + 1) * LANES]
+            at = (done // LANES + t) * SUB
+            out_ref[:, at : at + SUB, :] = tile.reshape(tile.shape[0] // SUB, SUB, LANES)
 
 
 def local_kernel(piece_rows, mid_ref, turn_ref, fh_ref, fl_ref, in_ref, out_ref, first, second):
@@ -180,34 +185,46 @@
             pltpu.VMEM((2 * span, LANES), jnp.float32),
             pltpu.VMEM((span, 2 * LANES), jnp.float32),
         ],
-        compiler_params=pltpu.CompilerParams(vmem_limit_bytes=48 << 20),
+        compiler_params=pltpu.CompilerParams(vmem_limit_bytes=20 << 20),
     )(mid, turn, fh, fl, arrived), kept
 
 
-def order_kernel(sources, in_ref, out_ref, whole):
+def order_kernel(sources, in_ref, out_ref, whole, ordered, sems):
     count = len(sources)
     fold = LANES // count
     each = in_ref.shape[0] // count
     tiles = each // SUB // fold
     lows = SUB // 2
+    rows = tiles * LANES * 2
     for k, at in enumerate(sources):
         whole[k * each : (k + 1) * each, :] = in_ref[at * each : (at + 1) * each, :]
-    for c in range(2):
-        for low in range(lows):
+    copies = []
+    for low in range(lows):
+        for c in range(2):
             for t in range(tiles):
                 parts = [
                     whole[pl.ds((v * tiles + t) * SUB + c * lows + low, count, each), :] for v in range(fold)
                 ]
-                base = (low * tiles + t) * LANES * 2 + c
-                out_ref[pl.ds(base, LANES, 2), :] = jnp.concatenate(parts, 0).T
+                ordered[pl.ds(low * rows + t * LANES * 2 + c, LANES, 2), :] = jnp.concatenate(parts, 0).T
+        piece = pl.ds(low * rows, rows)
+        copies.append(pltpu.make_async_copy(ordered.at[piece, :], out_ref.at[piece, :], sems.at[low]))
+        copies[-1].start()
+    for copy in copies:
+        copy.wait()
 
 
 def order_rows(landed, sources):
     return pl.pallas_call(
         functools.partial(order_kernel, sources),
+        in_specs=[pl.BlockSpec(memory_space=pltpu.VMEM)],
+        out_specs=pl.BlockSpec(memory_space=pltpu.HBM),
         out_shape=jax.ShapeDtypeStruct(landed.shape, jnp.float32),
-        scratch_shapes=[pltpu.VMEM(landed.shape, jnp.float32)],
-        compiler_params=pltpu.CompilerParams(vmem_limit_bytes=32 << 20),
+        scratch_shapes=[
+            pltpu.VMEM(landed.shape, jnp.float32),
+            pltpu.VMEM(landed.shape, jnp.float32),
+            pltpu.SemaphoreType.DMA((SUB // 2,)),
+        ],
+        compiler_params=pltpu.CompilerParams(vmem_limit_bytes=16 << 20),
     )(landed)
 
 
@@ -281,12 +298,12 @@
 def quarters(series, start, size):
     parts = pl.pallas_call(
         functools.partial(quarter_kernel, start),
-        in_specs=[pl.BlockSpec(memory_space=pl.ANY)],
+        in_specs=[pl.BlockSpec(memory_space=pltpu.HBM)],
         out_specs=[VMEM_WHOLE] * 4,
         out_shape=[jax.ShapeDtypeStruct((2, size), jnp.float32)] * 4,
         scratch_shapes=[pltpu.SemaphoreType.DMA((4,))],
-        compiler_params=pltpu.CompilerParams(vmem_limit_bytes=56 << 20),
-    )(series)
+        compiler_params=pltpu.CompilerParams(vmem_limit_bytes=8 << 20),
+    )(pltpu.with_memory_space_constraint(series, pltpu.HBM))
     return [part.reshape(2, size // LANES, LANES).transpose(1, 0, 2).reshape(-1, LANES) for part in parts]
 
 
@@ -389,22 +406,35 @@
             pltpu.VMEM((2048, LANES), jnp.float32),
             pltpu.VMEM((1024, 2 * LANES), jnp.float32),
         ],
-        compiler_params=pltpu.CompilerParams(vmem_limit_bytes=48 << 20),
+        compiler_params=pltpu.CompilerParams(vmem_limit_bytes=20 << 20),
     )(rows_of(bits), near, mid, turn, fh, fl, *arrived)
 
 
-CHUNKS = (128, 128)
+CHUNKS = (96, 160)
+
+
+def after(arrays, result):
+    return list(lax.optimization_barrier((*arrays, result)))[:-1]
 
 
 def by_axes(series, points):
     slab = series.shape[1]
+    starts = [sum(CHUNKS[:h]) for h in range(len(CHUNKS))]
+    tables = [mix_tables(points, start, rows) for start, rows in zip(starts, CHUNKS)]
+    one, two = [quarters(series, start * LANES, rows * LANES) for start, rows in zip(starts, CHUNKS)]
+    one = swap(one, 3)
+    two = swap(two, 3)
+    one = mix(one, (True,), tables[0][0])
+    one = swap(one, 1)
+    one = after(one, two[2])
+    one = mix(one, (False,) * (CHUNKS[0] // 32), tables[0][1])
+    one = swap(one, 3)
+    two = mix(two, (True,), tables[1][0])
+    two = swap(two, 1)
+    two = mix(two, (False,) * (CHUNKS[1] // 32), tables[1][1])
+    two = swap(two, 3)
     arrived = []
-    for h, rows in enumerate(CHUNKS):
-        start = sum(CHUNKS[:h])
-        first, second = mix_tables(points, start, rows)
-        parts = swap(quarters(series, start * LANES, rows * LANES), 3)
-        parts = swap(mix(parts, (True,), first), 1)
-        parts = swap(mix(parts, (False,) * (rows // 32), second), 3)
+    for parts in (one, two):
         mine = [parts[m] for m in FAR_FIRST]
         arrived += mine + [send(part, 1) for part in mine]
     dest, c, low = np.meshgrid(np.arange(32), np.arange(2), np.arange(4), indexing="ij")

time: 97.1 us -> 92.8 us (0.956)
  starting transfers between devices: 39.3 us -> 30.6 us
  waiting for transfers between devices: 16.3 us -> 23 us
  Pallas kernels: 10.2 us -> 7.12 us
  blocking collectives: 29.9 us -> 31.7 us
    ppermute x26, starting transfers between devices: 39.3 us -> 30.6 us  [send(): lax.ppermute(part, AXES, [(d, d ^ flip) for d in range(lax.axis_size(AXES...]
    ppermute x26, waiting for transfers between devices: 16.3 us -> 23 us  [send(): lax.ppermute(part, AXES, [(d, d ^ flip) for d in range(lax.axis_size(AXES...]
    all_to_all x1, blocking collectives: 29.9 us -> 31.7 us  [by_axes(): lax.all_to_all(spectrum, AXES, split_axis=0, concat_axis=0, tiled=True)]
    pallas_call x2, Pallas kernels: 3.95 us -> 2.38 us  [quarters(): pl.pallas_call(functools.partial(quarter_kernel, start), in_specs=[pl.Blo...]
    pallas_call x1, Pallas kernels: 3.56 us -> 2.25 us  [slab_transform(): pl.pallas_call(functools.partial(slab_kernel, starts), in_specs=[VMEM_WHO...]
  transfers between devices with their start and end apart: 26 -> 26, of which waited for: 8 -> 7; matrix products, arithmetic and copies ran while one was open for 0% -> 0% of each run, Pallas kernels for 3% -> 2%
where the time goes in v1:
time: 92.8 us; the launch traced here: 92.6 us
  blocking collectives  31.7 us (34%)
  starting transfers between devices  30.6 us (33%)
  waiting for transfers between devices  23 us (25%)
  Pallas kernels  7.12 us (8%)
    all_to_all x1, blocking collectives, by_axes(): lax.all_to_all(spectrum, AXES, split_axis=0, concat_axis=0, tiled=True)  31.7 us
    ppermute x26, starting transfers between devices, send(): lax.ppermute(part, AXES, [(d, d ^ flip) for d in range(lax.axis_size(AXES...  30.6 us
    ppermute x26, waiting for transfers between devices, send(): lax.ppermute(part, AXES, [(d, d ^ flip) for d in range(lax.axis_size(AXES...  23 us
    pallas_call x2, Pallas kernels, quarters(): pl.pallas_call(functools.partial(quarter_kernel, start), in_specs=[pl.Blo...  2.38 us
    pallas_call x1, Pallas kernels, slab_transform(): pl.pallas_call(functools.partial(slab_kernel, starts), in_specs=[VMEM_WHO...  2.25 us
  transfers between devices with their start and end apart: 26, of which 7 were waited for; matrix products, arithmetic and copies ran while one was open for 0% of the time, Pallas kernels for 2%

profile of v1, /device:TPU:0, one launch (start us, length us, event | category | flops | bytes accessed | tf_op | source)
XLA Modules:
  0.0 92.6 jit_solution(12965953915096729748)
XLA Ops:
  0.0 1.1 %shard_map.109 = (f32[2,12288]{1,0:T(2,128)S(1)}, f32[2,12288]{1,0:T(2,128)S(1)}, f32[2,12288]{1,0:T(2,128)S(1)}, f32[2,12288]{1,0:T(2,128)S(1)}) custom-call(f32[2,131072]{1,0:T(2,128)} %in_ref.3), custom_call_target="tpu_custom_call" | custom-call | tf_op jit(solution)/shard_map/pallas_call | solution.py:299
  1.1 4.1 %collective-permute-start = (f32[192,128]{1,0:T(8,128)S(1)}, f32[192,128]{1,0:T(8,128)S(1)}, u32[]{:S(2)}, u32[]{:S(2)}) collective-permute-start(f32[192,128]{1,0:T(8,128)S(1)} %bitcast.54), channel_id=1, source_target_pairs={{0,16},{1,17},{2,18},{3,19},{4,20},{5,21},{6,22},{7,23},{8,24},{9,... | collective-permute-start | bytes 294920 | tf_op jit(solution)/shard_map/ppermute | solution.py:315
  5.2 1.3 %collective-permute-start.1 = (f32[192,128]{1,0:T(8,128)S(1)}, f32[192,128]{1,0:T(8,128)S(1)}, u32[]{:S(2)}, u32[]{:S(2)}) collective-permute-start(f32[192,128]{1,0:T(8,128)S(1)} %bitcast.53), channel_id=1, source_target_pairs={{0,24},{1,25},{2,26},{3,27},{4,28},{5,29},{6,30},{7,31},{8,16},{9,... | collective-permute-start | bytes 294920 | tf_op jit(solution)/shard_map/ppermute | solution.py:315
  6.8 1.3 %shard_map.111 = (f32[2,20480]{1,0:T(2,128)S(1)}, f32[2,20480]{1,0:T(2,128)S(1)}, f32[2,20480]{1,0:T(2,128)S(1)}, f32[2,20480]{1,0:T(2,128)S(1)}) custom-call(f32[2,131072]{1,0:T(2,128)} %in_ref.3), custom_call_target="tpu_custom_call" | custom-call | tf_op jit(solution)/shard_map/pallas_call | solution.py:299
  8.1 2.9 %collective-permute-start.6 = (f32[320,128]{1,0:T(8,128)S(1)}, f32[320,128]{1,0:T(8,128)S(1)}, u32[]{:S(2)}, u32[]{:S(2)}) collective-permute-start(f32[320,128]{1,0:T(8,128)S(1)} %bitcast.51), channel_id=1, source_target_pairs={{0,16},{1,17},{2,18},{3,19},{4,20},{5,21},{6,22},{7,23},{8,24},{9,... | collective-permute-start | bytes 491528 | tf_op jit(solution)/shard_map/ppermute | solution.py:315
  11.0 1.3 %collective-permute-start.14 = (f32[320,128]{1,0:T(8,128)S(1)}, f32[320,128]{1,0:T(8,128)S(1)}, u32[]{:S(2)}, u32[]{:S(2)}) collective-permute-start(f32[320,128]{1,0:T(8,128)S(1)} %bitcast.50), channel_id=1, source_target_pairs={{0,24},{1,25},{2,26},{3,27},{4,28},{5,29},{6,30},{7,31},{8,16},{9,... | collective-permute-start | bytes 491528 | tf_op jit(solution)/shard_map/ppermute | solution.py:315
  12.3 2.0 %collective-permute-done.refs_1_ = f32[192,128]{1,0:T(8,128)S(1)} collective-permute-done((f32[192,128]{1,0:T(8,128)S(1)}, f32[192,128]{1,0:T(8,128)S(1)}, u32[]{:S(2)}, u32[]{:S(2)}) %collective-permute-start) | collective-permute-done | bytes 98336 | tf_op jit(solution)/shard_map/ppermute | solution.py:315
  14.5 2.0 %collective-permute-start.3 = (f32[192,128]{1,0:T(8,128)S(1)}, f32[192,128]{1,0:T(8,128)S(1)}, u32[]{:S(2)}, u32[]{:S(2)}) collective-permute-start(f32[192,128]{1,0:T(8,128)S(1)} %get-tuple-element.38), channel_id=1, source_target_pairs={{0,2},{1,3},{2,0},{3,1},{4,6},{5,7},{6,4},{7,5},{8,10},{9,11},{10,... | collective-permute-start | bytes 294920 | tf_op jit(solution)/shard_map/ppermute | solution.py:315
  16.5 1.5 %collective-permute-start.4 = (f32[192,128]{1,0:T(8,128)S(1)}, f32[192,128]{1,0:T(8,128)S(1)}, u32[]{:S(2)}, u32[]{:S(2)}) collective-permute-start(f32[192,128]{1,0:T(8,128)S(1)} %get-tuple-element.39), channel_id=1, source_target_pairs={{0,4},{1,5},{2,6},{3,7},{4,0},{5,1},{6,2},{7,3},{8,12},{9,13},{10,... | collective-permute-start | bytes 294920 | tf_op jit(solution)/shard_map/ppermute | solution.py:315
  18.0 7.7 %collective-permute-done.6.refs_1_ = f32[320,128]{1,0:T(8,128)S(1)} collective-permute-done((f32[320,128]{1,0:T(8,128)S(1)}, f32[320,128]{1,0:T(8,128)S(1)}, u32[]{:S(2)}, u32[]{:S(2)}) %collective-permute-start.6) | collective-permute-done | bytes 163872 | tf_op jit(solution)/shard_map/ppermute | solution.py:315
  25.7 2.7 %collective-permute-start.5 = (f32[192,128]{1,0:T(8,128)S(1)}, f32[192,128]{1,0:T(8,128)S(1)}, u32[]{:S(2)}, u32[]{:S(2)}) collective-permute-start(f32[192,128]{1,0:T(8,128)S(1)} %get-tuple-element.40), channel_id=1, source_target_pairs={{0,6},{1,7},{2,4},{3,5},{4,2},{5,3},{6,0},{7,1},{8,14},{9,15},{10,... | collective-permute-start | bytes 294920 | tf_op jit(solution)/shard_map/ppermute | solution.py:315
  28.7 0.6 collective-permute-start.16
  29.3 1.5 %collective-permute-start.17 = (f32[320,128]{1,0:T(8,128)S(1)}, f32[320,128]{1,0:T(8,128)S(1)}, u32[]{:S(2)}, u32[]{:S(2)}) collective-permute-start(f32[320,128]{1,0:T(8,128)S(1)} %get-tuple-element.55), channel_id=1, source_target_pairs={{0,6},{1,7},{2,4},{3,5},{4,2},{5,3},{6,0},{7,1},{8,14},{9,15},{10,... | collective-permute-start | bytes 491528 | tf_op jit(solution)/shard_map/ppermute | solution.py:315
  30.8 1.5 %collective-permute-start.18 = (f32[320,128]{1,0:T(8,128)S(1)}, f32[320,128]{1,0:T(8,128)S(1)}, u32[]{:S(2)}, u32[]{:S(2)}) collective-permute-start(f32[320,128]{1,0:T(8,128)S(1)} %get-tuple-element.56), channel_id=1, source_target_pairs={{0,2},{1,3},{2,0},{3,1},{4,6},{5,7},{6,4},{7,5},{8,10},{9,11},{10,... | collective-permute-start | bytes 491528 | tf_op jit(solution)/shard_map/ppermute | solution.py:315
  32.5 2.8 %collective-permute-start.7 = (f32[192,128]{1,0:T(8,128)S(1)}, f32[192,128]{1,0:T(8,128)S(1)}, u32[]{:S(2)}, u32[]{:S(2)}) collective-permute-start(f32[192,128]{1,0:T(8,128)S(1)} %get-tuple-element.47), channel_id=1, source_target_pairs={{0,16},{1,17},{2,18},{3,19},{4,20},{5,21},{6,22},{7,23},{8,24},{9,... | collective-permute-start | bytes 294920 | tf_op jit(solution)/shard_map/ppermute | solution.py:315
  35.7 1.5 %collective-permute-done.16.refs_1_ = f32[320,128]{1,0:T(8,128)S(1)} collective-permute-done((f32[320,128]{1,0:T(8,128)S(1)}, f32[320,128]{1,0:T(8,128)S(1)}, u32[]{:S(2)}, u32[]{:S(2)}) %collective-permute-start.16) | collective-permute-done | bytes 163872 | tf_op jit(solution)/shard_map/ppermute | solution.py:315
  37.3 2.0 %collective-permute-start.9 = (f32[192,128]{1,0:T(8,128)S(1)}, f32[192,128]{1,0:T(8,128)S(1)}, u32[]{:S(2)}, u32[]{:S(2)}) collective-permute-start(f32[192,128]{1,0:T(8,128)S(1)} %get-tuple-element.49), channel_id=1, source_target_pairs={{0,8},{1,9},{2,10},{3,11},{4,12},{5,13},{6,14},{7,15},{8,0},{9,1},... | collective-permute-start | bytes 294920 | tf_op jit(solution)/shard_map/ppermute | solution.py:315
  39.5 3.2 %collective-permute-start.19 = (f32[320,128]{1,0:T(8,128)S(1)}, f32[320,128]{1,0:T(8,128)S(1)}, u32[]{:S(2)}, u32[]{:S(2)}) collective-permute-start(f32[320,128]{1,0:T(8,128)S(1)} %get-tuple-element.58), channel_id=1, source_target_pairs={{0,16},{1,17},{2,18},{3,19},{4,20},{5,21},{6,22},{7,23},{8,24},{9,... | collective-permute-start | bytes 491528 | tf_op jit(solution)/shard_map/ppermute | solution.py:315
  44.1 0.8 collective-permute-done.10.refs_4_
  45.4 9.7 %collective-permute-done.19.refs_9_ = f32[320,128]{1,0:T(8,128)S(1)} collective-permute-done((f32[320,128]{1,0:T(8,128)S(1)}, f32[320,128]{1,0:T(8,128)S(1)}, u32[]{:S(2)}, u32[]{:S(2)}) %collective-permute-start.19) | collective-permute-done | bytes 163872 | tf_op jit(solution)/shard_map/ppermute | solution.py:315
  56.1 1.0 %collective-permute-done.13.refs_7_ = f32[192,128]{1,0:T(8,128)S(1)} collective-permute-done((f32[192,128]{1,0:T(8,128)S(1)}, f32[192,128]{1,0:T(8,128)S(1)}, u32[]{:S(2)}, u32[]{:S(2)}) %collective-permute-start.13) | collective-permute-done | bytes 98336 | tf_op jit(solution)/shard_map/ppermute | solution.py:315
  57.2 2.3 %shard_map.115 = f32[32,64,128]{2,1,0:T(8,128)S(1)} custom-call(f32[32,128]{1,0:T(8,128)S(1)} %copy-done.6, f32[2048,128]{1,0:T(8,128)S(1)} %copy-done.2, f32[2048,128]{1,0:T(8,128)S(1)} %copy-done.1, f32[2048,128]{1,0:T(8,128)S(1)} %copy-done, bf16[256,256]{1,0:T(8,128)(2,1)S(1)} %copy-done.4, bf16[256,256]{1,0:T(8,128)(2,1)S(1)} %copy-done.3, ...), custom_call_target="tpu_custom_call" | custom-call | tf_op jit(solution)/shard_map/pallas_call | solution.py:400
  59.4 31.7 %all_to_all.5 = f32[32,64,128]{2,1,0:T(8,128)S(1)} all-to-all(f32[32,64,128]{2,1,0:T(8,128)S(1)} %shard_map.115), channel_id=1, replica_groups=mesh['grp'=4,'dev'=8] {'grp','dev'}, dimensions={0} | all-to-all | bytes 2097152 | tf_op jit(solution)/shard_map/all_to_all | solution.py:443
  91.1 1.5 %shard_map.116 = f32[2048,128]{1,0:T(8,128)} custom-call(f32[2048,128]{1,0:T(8,128)S(1)} %bitcast.46), custom_call_target="tpu_custom_call" | custom-call | tf_op jit(solution)/shard_map/pallas_call | solution.py:217
  (55 shorter events, 4.6 us)
Async XLA Ops:
  1.1 13.2 %collective-permute-start = (f32[192,128]{1,0:T(8,128)S(1)}, f32[192,128]{1,0:T(8,128)S(1)}, u32[]{:S(2)}, u32[]{:S(2)}) collective-permute-start(f32[192,128]{1,0:T(8,128)S(1)} %bitcast.54), channel_id=1, source_target_pairs={{0,16},{1,17},{2,18},{3,19},{4,20},{5,21},{6,22},{7,23},{8,24},{9,... | collective-permute-start | bytes 294920 | tf_op jit(solution)/shard_map/ppermute | solution.py:315
  5.2 9.1 %collective-permute-start.1 = (f32[192,128]{1,0:T(8,128)S(1)}, f32[192,128]{1,0:T(8,128)S(1)}, u32[]{:S(2)}, u32[]{:S(2)}) collective-permute-start(f32[192,128]{1,0:T(8,128)S(1)} %bitcast.53), channel_id=1, source_target_pairs={{0,24},{1,25},{2,26},{3,27},{4,28},{5,29},{6,30},{7,31},{8,16},{9,... | collective-permute-start | bytes 294920 | tf_op jit(solution)/shard_map/ppermute | solution.py:315
  6.6 7.7 %collective-permute-start.2 = (f32[192,128]{1,0:T(8,128)S(1)}, f32[192,128]{1,0:T(8,128)S(1)}, u32[]{:S(2)}, u32[]{:S(2)}) collective-permute-start(f32[192,128]{1,0:T(8,128)S(1)} %bitcast.52), channel_id=1, source_target_pairs={{0,8},{1,9},{2,10},{3,11},{4,12},{5,13},{6,14},{7,15},{8,0},{9,1},... | collective-permute-start | bytes 294920 | tf_op jit(solution)/shard_map/ppermute | solution.py:315
  8.1 17.7 %collective-permute-start.6 = (f32[320,128]{1,0:T(8,128)S(1)}, f32[320,128]{1,0:T(8,128)S(1)}, u32[]{:S(2)}, u32[]{:S(2)}) collective-permute-start(f32[320,128]{1,0:T(8,128)S(1)} %bitcast.51), channel_id=1, source_target_pairs={{0,16},{1,17},{2,18},{3,19},{4,20},{5,21},{6,22},{7,23},{8,24},{9,... | collective-permute-start | bytes 491528 | tf_op jit(solution)/shard_map/ppermute | solution.py:315
  11.0 17.4 %collective-permute-start.14 = (f32[320,128]{1,0:T(8,128)S(1)}, f32[320,128]{1,0:T(8,128)S(1)}, u32[]{:S(2)}, u32[]{:S(2)}) collective-permute-start(f32[320,128]{1,0:T(8,128)S(1)} %bitcast.50), channel_id=1, source_target_pairs={{0,24},{1,25},{2,26},{3,27},{4,28},{5,29},{6,30},{7,31},{8,16},{9,... | collective-permute-start | bytes 491528 | tf_op jit(solution)/shard_map/ppermute | solution.py:315
  14.3 14.1 %collective-permute-start.15 = (f32[320,128]{1,0:T(8,128)S(1)}, f32[320,128]{1,0:T(8,128)S(1)}, u32[]{:S(2)}, u32[]{:S(2)}) collective-permute-start(f32[320,128]{1,0:T(8,128)S(1)} %bitcast.49), channel_id=1, source_target_pairs={{0,8},{1,9},{2,10},{3,11},{4,12},{5,13},{6,14},{7,15},{8,0},{9,1},... | collective-permute-start | bytes 491528 | tf_op jit(solution)/shard_map/ppermute | solution.py:315
  14.5 16.2 %collective-permute-start.3 = (f32[192,128]{1,0:T(8,128)S(1)}, f32[192,128]{1,0:T(8,128)S(1)}, u32[]{:S(2)}, u32[]{:S(2)}) collective-permute-start(f32[192,128]{1,0:T(8,128)S(1)} %get-tuple-element.38), channel_id=1, source_target_pairs={{0,2},{1,3},{2,0},{3,1},{4,6},{5,7},{6,4},{7,5},{8,10},{9,11},{10,... | collective-permute-start | bytes 294920 | tf_op jit(solution)/shard_map/ppermute | solution.py:315
  16.5 15.7 %collective-permute-start.4 = (f32[192,128]{1,0:T(8,128)S(1)}, f32[192,128]{1,0:T(8,128)S(1)}, u32[]{:S(2)}, u32[]{:S(2)}) collective-permute-start(f32[192,128]{1,0:T(8,128)S(1)} %get-tuple-element.39), channel_id=1, source_target_pairs={{0,4},{1,5},{2,6},{3,7},{4,0},{5,1},{6,2},{7,3},{8,12},{9,13},{10,... | collective-permute-start | bytes 294920 | tf_op jit(solution)/shard_map/ppermute | solution.py:315
  25.7 6.5 %collective-permute-start.5 = (f32[192,128]{1,0:T(8,128)S(1)}, f32[192,128]{1,0:T(8,128)S(1)}, u32[]{:S(2)}, u32[]{:S(2)}) collective-permute-start(f32[192,128]{1,0:T(8,128)S(1)} %get-tuple-element.40), channel_id=1, source_target_pairs={{0,6},{1,7},{2,4},{3,5},{4,2},{5,3},{6,0},{7,1},{8,14},{9,15},{10,... | collective-permute-start | bytes 294920 | tf_op jit(solution)/shard_map/ppermute | solution.py:315
  28.7 8.6 %collective-permute-start.16 = (f32[320,128]{1,0:T(8,128)S(1)}, f32[320,128]{1,0:T(8,128)S(1)}, u32[]{:S(2)}, u32[]{:S(2)}) collective-permute-start(f32[320,128]{1,0:T(8,128)S(1)} %get-tuple-element.54), channel_id=1, source_target_pairs={{0,4},{1,5},{2,6},{3,7},{4,0},{5,1},{6,2},{7,3},{8,12},{9,13},{10,... | collective-permute-start | bytes 491528 | tf_op jit(solution)/shard_map/ppermute | solution.py:315
  29.3 10.0 %collective-permute-start.17 = (f32[320,128]{1,0:T(8,128)S(1)}, f32[320,128]{1,0:T(8,128)S(1)}, u32[]{:S(2)}, u32[]{:S(2)}) collective-permute-start(f32[320,128]{1,0:T(8,128)S(1)} %get-tuple-element.55), channel_id=1, source_target_pairs={{0,6},{1,7},{2,4},{3,5},{4,2},{5,3},{6,0},{7,1},{8,14},{9,15},{10,... | collective-permute-start | bytes 491528 | tf_op jit(solution)/shard_map/ppermute | solution.py:315
  30.8 8.5 %collective-permute-start.18 = (f32[320,128]{1,0:T(8,128)S(1)}, f32[320,128]{1,0:T(8,128)S(1)}, u32[]{:S(2)}, u32[]{:S(2)}) collective-permute-start(f32[320,128]{1,0:T(8,128)S(1)} %get-tuple-element.56), channel_id=1, source_target_pairs={{0,2},{1,3},{2,0},{3,1},{4,6},{5,7},{6,4},{7,5},{8,10},{9,11},{10,... | collective-permute-start | bytes 491528 | tf_op jit(solution)/shard_map/ppermute | solution.py:315
  32.5 10.7 %collective-permute-start.7 = (f32[192,128]{1,0:T(8,128)S(1)}, f32[192,128]{1,0:T(8,128)S(1)}, u32[]{:S(2)}, u32[]{:S(2)}) collective-permute-start(f32[192,128]{1,0:T(8,128)S(1)} %get-tuple-element.47), channel_id=1, source_target_pairs={{0,16},{1,17},{2,18},{3,19},{4,20},{5,21},{6,22},{7,23},{8,24},{9,... | collective-permute-start | bytes 294920 | tf_op jit(solution)/shard_map/ppermute | solution.py:315
  35.3 8.3 %collective-permute-start.8 = (f32[192,128]{1,0:T(8,128)S(1)}, f32[192,128]{1,0:T(8,128)S(1)}, u32[]{:S(2)}, u32[]{:S(2)}) collective-permute-start(f32[192,128]{1,0:T(8,128)S(1)} %get-tuple-element.48), channel_id=1, source_target_pairs={{0,24},{1,25},{2,26},{3,27},{4,28},{5,29},{6,30},{7,31},{8,16},{9,... | collective-permute-start | bytes 294920 | tf_op jit(solution)/shard_map/ppermute | solution.py:315
  37.3 6.5 %collective-permute-start.9 = (f32[192,128]{1,0:T(8,128)S(1)}, f32[192,128]{1,0:T(8,128)S(1)}, u32[]{:S(2)}, u32[]{:S(2)}) collective-permute-start(f32[192,128]{1,0:T(8,128)S(1)} %get-tuple-element.49), channel_id=1, source_target_pairs={{0,8},{1,9},{2,10},{3,11},{4,12},{5,13},{6,14},{7,15},{8,0},{9,1},... | collective-permute-start | bytes 294920 | tf_op jit(solution)/shard_map/ppermute | solution.py:315
  39.5 15.5 %collective-permute-start.19 = (f32[320,128]{1,0:T(8,128)S(1)}, f32[320,128]{1,0:T(8,128)S(1)}, u32[]{:S(2)}, u32[]{:S(2)}) collective-permute-start(f32[320,128]{1,0:T(8,128)S(1)} %get-tuple-element.58), channel_id=1, source_target_pairs={{0,16},{1,17},{2,18},{3,19},{4,20},{5,21},{6,22},{7,23},{8,24},{9,... | collective-permute-start | bytes 491528 | tf_op jit(solution)/shard_map/ppermute | solution.py:315
  42.7 12.3 %collective-permute-start.20 = (f32[320,128]{1,0:T(8,128)S(1)}, f32[320,128]{1,0:T(8,128)S(1)}, u32[]{:S(2)}, u32[]{:S(2)}) collective-permute-start(f32[320,128]{1,0:T(8,128)S(1)} %get-tuple-element.59), channel_id=1, source_target_pairs={{0,24},{1,25},{2,26},{3,27},{4,28},{5,29},{6,30},{7,31},{8,16},{9,... | collective-permute-start | bytes 491528 | tf_op jit(solution)/shard_map/ppermute | solution.py:315
  43.2 12.4 %collective-permute-start.21 = (f32[320,128]{1,0:T(8,128)S(1)}, f32[320,128]{1,0:T(8,128)S(1)}, u32[]{:S(2)}, u32[]{:S(2)}) collective-permute-start(f32[320,128]{1,0:T(8,128)S(1)} %get-tuple-element.60), channel_id=1, source_target_pairs={{0,8},{1,9},{2,10},{3,11},{4,12},{5,13},{6,14},{7,15},{8,0},{9,1},... | collective-permute-start | bytes 491528 | tf_op jit(solution)/shard_map/ppermute | solution.py:315
  44.8 10.8 %collective-permute-start.12 = (f32[192,128]{1,0:T(8,128)S(1)}, f32[192,128]{1,0:T(8,128)S(1)}, u32[]{:S(2)}, u32[]{:S(2)}) collective-permute-start(f32[192,128]{1,0:T(8,128)S(1)} %collective-permute-done.8.refs_2_), channel_id=1, source_target_pairs={{0,1},{1,0},{2,3},{3,2},{4,5},{5,4},{6,7},{7,6},{8,9},{9,8},{10,11... | collective-permute-start | bytes 294920 | tf_op jit(solution)/shard_map/ppermute | solution.py:315
  45.0 12.1 %collective-permute-start.22 = (f32[320,128]{1,0:T(8,128)S(1)}, f32[320,128]{1,0:T(8,128)S(1)}, u32[]{:S(2)}, u32[]{:S(2)}) collective-permute-start(f32[320,128]{1,0:T(8,128)S(1)} %get-tuple-element.57.refs_8_), channel_id=1, source_target_pairs={{0,1},{1,0},{2,3},{3,2},{4,5},{5,4},{6,7},{7,6},{8,9},{9,8},{10,11... | collective-permute-start | bytes 491528 | tf_op jit(solution)/shard_map/ppermute | solution.py:315
  55.0 2.1 %collective-permute-start.23 = (f32[320,128]{1,0:T(8,128)S(1)}, f32[320,128]{1,0:T(8,128)S(1)}, u32[]{:S(2)}, u32[]{:S(2)}) collective-permute-start(f32[320,128]{1,0:T(8,128)S(1)} %collective-permute-done.19.refs_9_), channel_id=1, source_target_pairs={{0,1},{1,0},{2,3},{3,2},{4,5},{5,4},{6,7},{7,6},{8,9},{9,8},{10,11... | collective-permute-start | bytes 491528 | tf_op jit(solution)/shard_map/ppermute | solution.py:315
  55.0 2.1 %collective-permute-start.24 = (f32[320,128]{1,0:T(8,128)S(1)}, f32[320,128]{1,0:T(8,128)S(1)}, u32[]{:S(2)}, u32[]{:S(2)}) collective-permute-start(f32[320,128]{1,0:T(8,128)S(1)} %collective-permute-done.20.refs_10_), channel_id=1, source_target_pairs={{0,1},{1,0},{2,3},{3,2},{4,5},{5,4},{6,7},{7,6},{8,9},{9,8},{10,11... | collective-permute-start | bytes 491528 | tf_op jit(solution)/shard_map/ppermute | solution.py:315
  55.6 1.6 %collective-permute-start.25 = (f32[320,128]{1,0:T(8,128)S(1)}, f32[320,128]{1,0:T(8,128)S(1)}, u32[]{:S(2)}, u32[]{:S(2)}) collective-permute-start(f32[320,128]{1,0:T(8,128)S(1)} %collective-permute-done.21.refs_11_), channel_id=1, source_target_pairs={{0,1},{1,0},{2,3},{3,2},{4,5},{5,4},{6,7},{7,6},{8,9},{9,8},{10,11... | collective-permute-start | bytes 491528 | tf_op jit(solution)/shard_map/ppermute | solution.py:315
  55.6 1.5 %collective-permute-start.13 = (f32[192,128]{1,0:T(8,128)S(1)}, f32[192,128]{1,0:T(8,128)S(1)}, u32[]{:S(2)}, u32[]{:S(2)}) collective-permute-start(f32[192,128]{1,0:T(8,128)S(1)} %collective-permute-done.9.refs_3_), channel_id=1, source_target_pairs={{0,1},{1,0},{2,3},{3,2},{4,5},{5,4},{6,7},{7,6},{8,9},{9,8},{10,11... | collective-permute-start | bytes 294920 | tf_op jit(solution)/shard_map/ppermute | solution.py:315
  (11 other events, 336.4 us)

commit v2 on v1

--- a/solution.py
+++ b/solution.py
@@ -106,9 +106,13 @@
     return high, (values - high.astype(jnp.float32)).astype(jnp.bfloat16)
 
 
+def first_pitch(outer, inner):
+    return outer // SUB * inner + SUB
+
+
 def lane_stage(outer, inner, turn_ref, fh_ref, fl_ref, out_ref, first, second):
     span = outer * inner
-    fold = outer // SUB
+    fold, pitch = outer // SUB, first_pitch(outer, inner)
     together = max(1, LANES // (inner * SUB))
     dot = functools.partial(
         lax.dot_general, dimension_numbers=(((1,), (1,)), ((), ())), preferred_element_type=jnp.float32
@@ -117,13 +121,8 @@
         for v in range(begin, begin + together):
             values = []
             for j in range(inner):
-                base = v * inner + j
-                values.append(
-                    (
-                        first[pl.ds(base, SUB, fold * inner), :],
-                        first[pl.ds(span + base, SUB, fold * inner), :],
-                    )
-                )
+                at = v * inner + j
+                values.append((first[pl.ds(at, SUB, pitch), :], first[pl.ds(SUB * pitch + at, SUB, pitch), :]))
             for k, (re, im) in enumerate(dft_list(values)):
                 base = (v * inner + k) * SUB
                 c, s = turn_ref[base : base + SUB, :], turn_ref[span + base : span + base + SUB, :]
@@ -143,6 +142,7 @@
     inner = piece_rows
     outer = in_ref.shape[0] // 2 // inner
     span = outer * inner
+    fold, pitch = outer // SUB, first_pitch(outer, inner)
     for j in range(0, inner, SUB):
         take = min(SUB, inner - j)
         values = []
@@ -152,8 +152,9 @@
         for k, (re, im) in enumerate(dft_list(values)):
             base = k * inner + j
             c, s = mid_ref[base : base + take, :], mid_ref[span + base : span + base + take, :]
-            first[base : base + take, :] = re * c - im * s
-            first[span + base : span + base + take, :] = re * s + im * c
+            at = k // fold * pitch + k % fold * inner + j
+            first[at : at + take, :] = re * c - im * s
+            first[SUB * pitch + at : SUB * pitch + at + take, :] = re * s + im * c
     lane_stage(outer, inner, turn_ref, fh_ref, fl_ref, out_ref, first, second)
 
 
@@ -182,7 +183,7 @@
         functools.partial(local_kernel, inner),
         out_shape=jax.ShapeDtypeStruct((2 * LANES // SUB, SUB * span // LANES, LANES), jnp.float32),
         scratch_shapes=[
-            pltpu.VMEM((2 * span, LANES), jnp.float32),
+            pltpu.VMEM((2 * SUB * first_pitch(outer, inner), LANES), jnp.float32),
             pltpu.VMEM((span, 2 * LANES), jnp.float32),
         ],
         compiler_params=pltpu.CompilerParams(vmem_limit_bytes=20 << 20),
@@ -196,19 +197,21 @@
     tiles = each // SUB // fold
     lows = SUB // 2
     rows = tiles * LANES * 2
+    pitch = each + SUB
     for k, at in enumerate(sources):
-        whole[k * each : (k + 1) * each, :] = in_ref[at * each : (at + 1) * each, :]
+        whole[k * pitch : k * pitch + each, :] = in_ref[at * each : (at + 1) * each, :]
     copies = []
     for low in range(lows):
-        for c in range(2):
-            for t in range(tiles):
+        for t in range(tiles):
+            base = low * rows + t * LANES * 2
+            for c in range(2):
                 parts = [
-                    whole[pl.ds((v * tiles + t) * SUB + c * lows + low, count, each), :] for v in range(fold)
+                    whole[pl.ds((v * tiles + t) * SUB + c * lows + low, count, pitch), :] for v in range(fold)
                 ]
-                ordered[pl.ds(low * rows + t * LANES * 2 + c, LANES, 2), :] = jnp.concatenate(parts, 0).T
-        piece = pl.ds(low * rows, rows)
-        copies.append(pltpu.make_async_copy(ordered.at[piece, :], out_ref.at[piece, :], sems.at[low]))
-        copies[-1].start()
+                ordered[pl.ds(base + c, LANES, 2), :] = jnp.concatenate(parts, 0).T
+            piece = pl.ds(base, LANES * 2)
+            copies.append(pltpu.make_async_copy(ordered.at[piece, :], out_ref.at[piece, :], sems.at[low, t]))
+            copies[-1].start()
     for copy in copies:
         copy.wait()
 
@@ -220,9 +223,9 @@
         out_specs=pl.BlockSpec(memory_space=pltpu.HBM),
         out_shape=jax.ShapeDtypeStruct(landed.shape, jnp.float32),
         scratch_shapes=[
+            pltpu.VMEM((landed.shape[0] + SUB * len(sources), LANES), jnp.float32),
             pltpu.VMEM(landed.shape, jnp.float32),
-            pltpu.VMEM(landed.shape, jnp.float32),
-            pltpu.SemaphoreType.DMA((SUB // 2,)),
+            pltpu.SemaphoreType.DMA((SUB // 2, landed.shape[0] // SUB // LANES)),
         ],
         compiler_params=pltpu.CompilerParams(vmem_limit_bytes=16 << 20),
     )(landed)
@@ -371,6 +374,7 @@
                     whole[pl.ds(at + r, SUB), :] = re * c - im * s
                     whole[pl.ds(span + at + r, SUB), :] = re * s + im * c
     outer = inner = 32
+    fold, pitch = outer // SUB, first_pitch(outer, inner)
     for j in range(0, inner, SUB):
         values = []
         for e in range(outer):
@@ -382,8 +386,9 @@
             base = k * inner + j
             mc, ms = mid_ref[base : base + SUB, :], mid_ref[span + base : span + base + SUB, :]
             c, s = mc * nc - ms * ns, mc * ns + ms * nc
-            first[base : base + SUB, :] = re * c - im * s
-            first[span + base : span + base + SUB, :] = re * s + im * c
+            at = k // fold * pitch + k % fold * inner + j
+            first[at : at + SUB, :] = re * c - im * s
+            first[SUB * pitch + at : SUB * pitch + at + SUB, :] = re * s + im * c
     lane_stage(outer, inner, turn_ref, fh_ref, fl_ref, out_ref, first, second)
 
 
@@ -403,7 +408,7 @@
         out_shape=jax.ShapeDtypeStruct((32, 64, LANES), jnp.float32),
         scratch_shapes=[
             pltpu.VMEM((2048, LANES), jnp.float32),
-            pltpu.VMEM((2048, LANES), jnp.float32),
+            pltpu.VMEM((2 * SUB * first_pitch(32, 32), LANES), jnp.float32),
             pltpu.VMEM((1024, 2 * LANES), jnp.float32),
         ],
         compiler_params=pltpu.CompilerParams(vmem_limit_bytes=20 << 20),
@@ -437,11 +442,12 @@
     for parts in (one, two):
         mine = [parts[m] for m in FAR_FIRST]
         arrived += mine + [send(part, 1) for part in mine]
-    dest, c, low = np.meshgrid(np.arange(32), np.arange(2), np.arange(4), indexing="ij")
+    at = np.arange(32).reshape(8, 4).T.reshape(-1)
+    dest, c, low = np.meshgrid(np.argsort(at), np.arange(2), np.arange(4), indexing="ij")
     lane_rows = ((dest * 4 + low).reshape(-1), (c == 1).reshape(-1))
     spectrum = slab_transform(arrived, lane_rows, points)
-    landed = lax.all_to_all(spectrum, AXES, split_axis=0, concat_axis=0, tiled=True).reshape(2048, LANES)
-    ordered = order_rows(landed, np.argsort(device_digits()[3]).tolist())
+    landed = lax.all_to_all(spectrum, ORDER, split_axis=0, concat_axis=0, tiled=True).reshape(2048, LANES)
+    ordered = order_rows(landed, at[np.argsort(device_digits()[3])].tolist())
     return ordered.reshape(slab // LANES, 2, LANES).transpose(1, 0, 2).reshape(2, slab)
 
 

time: 92.8 us -> 92 us (level); the launches traced: 92.6 us -> 90.7 us
  blocking collectives: 31.7 us -> 30.5 us
    all_to_all x1, blocking collectives: 31.7 us -> 30.5 us  [by_axes(): lax.all_to_all(spectrum, ORDER, split_axis=0, concat_axis=0, tiled=True)]
where the time goes in v2:
time: 92 us; the launch traced here: 90.7 us
  starting transfers between devices  30.6 us (33%)
  blocking collectives  30.5 us (33%)
  waiting for transfers between devices  23 us (25%)
  Pallas kernels  6.34 us (7%)
    ppermute x26, starting transfers between devices, send(): lax.ppermute(part, AXES, [(d, d ^ flip) for d in range(lax.axis_size(AXES...  30.6 us
    all_to_all x1, blocking collectives, by_axes(): lax.all_to_all(spectrum, ORDER, split_axis=0, concat_axis=0, tiled=True)  30.5 us
    ppermute x26, waiting for transfers between devices, send(): lax.ppermute(part, AXES, [(d, d ^ flip) for d in range(lax.axis_size(AXES...  23 us
    pallas_call x2, Pallas kernels, quarters(): pl.pallas_call(functools.partial(quarter_kernel, start), in_specs=[pl.Blo...  2.38 us
  transfers between devices with their start and end apart: 26, of which 7 were waited for; matrix products, arithmetic and copies ran while one was open for 0% of the time, Pallas kernels for 2%

profile of v2, /device:TPU:0, one launch (start us, length us, event | category | flops | bytes accessed | tf_op | source)
XLA Modules:
  0.0 90.7 jit_solution(15882937459525564919)
XLA Ops:
  0.0 1.1 %shard_map.109 = (f32[2,12288]{1,0:T(2,128)S(1)}, f32[2,12288]{1,0:T(2,128)S(1)}, f32[2,12288]{1,0:T(2,128)S(1)}, f32[2,12288]{1,0:T(2,128)S(1)}) custom-call(f32[2,131072]{1,0:T(2,128)} %in_ref.3), custom_call_target="tpu_custom_call" | custom-call | tf_op jit(solution)/shard_map/pallas_call | solution.py:302
  1.1 4.1 %collective-permute-start = (f32[192,128]{1,0:T(8,128)S(1)}, f32[192,128]{1,0:T(8,128)S(1)}, u32[]{:S(2)}, u32[]{:S(2)}) collective-permute-start(f32[192,128]{1,0:T(8,128)S(1)} %bitcast.54), channel_id=1, source_target_pairs={{0,16},{1,17},{2,18},{3,19},{4,20},{5,21},{6,22},{7,23},{8,24},{9,... | collective-permute-start | bytes 294920 | tf_op jit(solution)/shard_map/ppermute | solution.py:318
  5.2 1.3 %collective-permute-start.1 = (f32[192,128]{1,0:T(8,128)S(1)}, f32[192,128]{1,0:T(8,128)S(1)}, u32[]{:S(2)}, u32[]{:S(2)}) collective-permute-start(f32[192,128]{1,0:T(8,128)S(1)} %bitcast.53), channel_id=1, source_target_pairs={{0,24},{1,25},{2,26},{3,27},{4,28},{5,29},{6,30},{7,31},{8,16},{9,... | collective-permute-start | bytes 294920 | tf_op jit(solution)/shard_map/ppermute | solution.py:318
  6.8 1.3 %shard_map.111 = (f32[2,20480]{1,0:T(2,128)S(1)}, f32[2,20480]{1,0:T(2,128)S(1)}, f32[2,20480]{1,0:T(2,128)S(1)}, f32[2,20480]{1,0:T(2,128)S(1)}) custom-call(f32[2,131072]{1,0:T(2,128)} %in_ref.3), custom_call_target="tpu_custom_call" | custom-call | tf_op jit(solution)/shard_map/pallas_call | solution.py:302
  8.1 2.9 %collective-permute-start.6 = (f32[320,128]{1,0:T(8,128)S(1)}, f32[320,128]{1,0:T(8,128)S(1)}, u32[]{:S(2)}, u32[]{:S(2)}) collective-permute-start(f32[320,128]{1,0:T(8,128)S(1)} %bitcast.51), channel_id=1, source_target_pairs={{0,16},{1,17},{2,18},{3,19},{4,20},{5,21},{6,22},{7,23},{8,24},{9,... | collective-permute-start | bytes 491528 | tf_op jit(solution)/shard_map/ppermute | solution.py:318
  11.0 1.3 %collective-permute-start.14 = (f32[320,128]{1,0:T(8,128)S(1)}, f32[320,128]{1,0:T(8,128)S(1)}, u32[]{:S(2)}, u32[]{:S(2)}) collective-permute-start(f32[320,128]{1,0:T(8,128)S(1)} %bitcast.50), channel_id=1, source_target_pairs={{0,24},{1,25},{2,26},{3,27},{4,28},{5,29},{6,30},{7,31},{8,16},{9,... | collective-permute-start | bytes 491528 | tf_op jit(solution)/shard_map/ppermute | solution.py:318
  12.3 2.0 %collective-permute-done.refs_1_ = f32[192,128]{1,0:T(8,128)S(1)} collective-permute-done((f32[192,128]{1,0:T(8,128)S(1)}, f32[192,128]{1,0:T(8,128)S(1)}, u32[]{:S(2)}, u32[]{:S(2)}) %collective-permute-start) | collective-permute-done | bytes 98336 | tf_op jit(solution)/shard_map/ppermute | solution.py:318
  14.5 2.0 %collective-permute-start.3 = (f32[192,128]{1,0:T(8,128)S(1)}, f32[192,128]{1,0:T(8,128)S(1)}, u32[]{:S(2)}, u32[]{:S(2)}) collective-permute-start(f32[192,128]{1,0:T(8,128)S(1)} %get-tuple-element.38), channel_id=1, source_target_pairs={{0,2},{1,3},{2,0},{3,1},{4,6},{5,7},{6,4},{7,5},{8,10},{9,11},{10,... | collective-permute-start | bytes 294920 | tf_op jit(solution)/shard_map/ppermute | solution.py:318
  16.5 1.5 %collective-permute-start.4 = (f32[192,128]{1,0:T(8,128)S(1)}, f32[192,128]{1,0:T(8,128)S(1)}, u32[]{:S(2)}, u32[]{:S(2)}) collective-permute-start(f32[192,128]{1,0:T(8,128)S(1)} %get-tuple-element.39), channel_id=1, source_target_pairs={{0,4},{1,5},{2,6},{3,7},{4,0},{5,1},{6,2},{7,3},{8,12},{9,13},{10,... | collective-permute-start | bytes 294920 | tf_op jit(solution)/shard_map/ppermute | solution.py:318
  18.0 7.7 %collective-permute-done.6.refs_1_ = f32[320,128]{1,0:T(8,128)S(1)} collective-permute-done((f32[320,128]{1,0:T(8,128)S(1)}, f32[320,128]{1,0:T(8,128)S(1)}, u32[]{:S(2)}, u32[]{:S(2)}) %collective-permute-start.6) | collective-permute-done | bytes 163872 | tf_op jit(solution)/shard_map/ppermute | solution.py:318
  25.7 2.7 %collective-permute-start.5 = (f32[192,128]{1,0:T(8,128)S(1)}, f32[192,128]{1,0:T(8,128)S(1)}, u32[]{:S(2)}, u32[]{:S(2)}) collective-permute-start(f32[192,128]{1,0:T(8,128)S(1)} %get-tuple-element.40), channel_id=1, source_target_pairs={{0,6},{1,7},{2,4},{3,5},{4,2},{5,3},{6,0},{7,1},{8,14},{9,15},{10,... | collective-permute-start | bytes 294920 | tf_op jit(solution)/shard_map/ppermute | solution.py:318
  28.7 0.6 collective-permute-start.16
  29.3 1.5 %collective-permute-start.17 = (f32[320,128]{1,0:T(8,128)S(1)}, f32[320,128]{1,0:T(8,128)S(1)}, u32[]{:S(2)}, u32[]{:S(2)}) collective-permute-start(f32[320,128]{1,0:T(8,128)S(1)} %get-tuple-element.55), channel_id=1, source_target_pairs={{0,6},{1,7},{2,4},{3,5},{4,2},{5,3},{6,0},{7,1},{8,14},{9,15},{10,... | collective-permute-start | bytes 491528 | tf_op jit(solution)/shard_map/ppermute | solution.py:318
  30.8 1.5 %collective-permute-start.18 = (f32[320,128]{1,0:T(8,128)S(1)}, f32[320,128]{1,0:T(8,128)S(1)}, u32[]{:S(2)}, u32[]{:S(2)}) collective-permute-start(f32[320,128]{1,0:T(8,128)S(1)} %get-tuple-element.56), channel_id=1, source_target_pairs={{0,2},{1,3},{2,0},{3,1},{4,6},{5,7},{6,4},{7,5},{8,10},{9,11},{10,... | collective-permute-start | bytes 491528 | tf_op jit(solution)/shard_map/ppermute | solution.py:318
  32.5 2.8 %collective-permute-start.7 = (f32[192,128]{1,0:T(8,128)S(1)}, f32[192,128]{1,0:T(8,128)S(1)}, u32[]{:S(2)}, u32[]{:S(2)}) collective-permute-start(f32[192,128]{1,0:T(8,128)S(1)} %get-tuple-element.47), channel_id=1, source_target_pairs={{0,16},{1,17},{2,18},{3,19},{4,20},{5,21},{6,22},{7,23},{8,24},{9,... | collective-permute-start | bytes 294920 | tf_op jit(solution)/shard_map/ppermute | solution.py:318
  35.7 1.5 %collective-permute-done.16.refs_1_ = f32[320,128]{1,0:T(8,128)S(1)} collective-permute-done((f32[320,128]{1,0:T(8,128)S(1)}, f32[320,128]{1,0:T(8,128)S(1)}, u32[]{:S(2)}, u32[]{:S(2)}) %collective-permute-start.16) | collective-permute-done | bytes 163872 | tf_op jit(solution)/shard_map/ppermute | solution.py:318
  37.3 2.0 %collective-permute-start.9 = (f32[192,128]{1,0:T(8,128)S(1)}, f32[192,128]{1,0:T(8,128)S(1)}, u32[]{:S(2)}, u32[]{:S(2)}) collective-permute-start(f32[192,128]{1,0:T(8,128)S(1)} %get-tuple-element.49), channel_id=1, source_target_pairs={{0,8},{1,9},{2,10},{3,11},{4,12},{5,13},{6,14},{7,15},{8,0},{9,1},... | collective-permute-start | bytes 294920 | tf_op jit(solution)/shard_map/ppermute | solution.py:318
  39.5 3.2 %collective-permute-start.19 = (f32[320,128]{1,0:T(8,128)S(1)}, f32[320,128]{1,0:T(8,128)S(1)}, u32[]{:S(2)}, u32[]{:S(2)}) collective-permute-start(f32[320,128]{1,0:T(8,128)S(1)} %get-tuple-element.58), channel_id=1, source_target_pairs={{0,16},{1,17},{2,18},{3,19},{4,20},{5,21},{6,22},{7,23},{8,24},{9,... | collective-permute-start | bytes 491528 | tf_op jit(solution)/shard_map/ppermute | solution.py:318
  44.1 0.8 collective-permute-done.10.refs_4_
  45.4 9.7 %collective-permute-done.19.refs_9_ = f32[320,128]{1,0:T(8,128)S(1)} collective-permute-done((f32[320,128]{1,0:T(8,128)S(1)}, f32[320,128]{1,0:T(8,128)S(1)}, u32[]{:S(2)}, u32[]{:S(2)}) %collective-permute-start.19) | collective-permute-done | bytes 163872 | tf_op jit(solution)/shard_map/ppermute | solution.py:318
  56.1 1.0 %collective-permute-done.13.refs_7_ = f32[192,128]{1,0:T(8,128)S(1)} collective-permute-done((f32[192,128]{1,0:T(8,128)S(1)}, f32[192,128]{1,0:T(8,128)S(1)}, u32[]{:S(2)}, u32[]{:S(2)}) %collective-permute-start.13) | collective-permute-done | bytes 98336 | tf_op jit(solution)/shard_map/ppermute | solution.py:318
  57.2 1.8 %shard_map.115 = f32[32,64,128]{2,1,0:T(8,128)S(1)} custom-call(f32[32,128]{1,0:T(8,128)S(1)} %copy-done.6, f32[2048,128]{1,0:T(8,128)S(1)} %copy-done.2, f32[2048,128]{1,0:T(8,128)S(1)} %copy-done.1, f32[2048,128]{1,0:T(8,128)S(1)} %copy-done, bf16[256,256]{1,0:T(8,128)(2,1)S(1)} %copy-done.4, bf16[256,256]{1,0:T(8,128)(2,1)S(1)} %copy-done.3, ...), custom_call_target="tpu_custom_call" | custom-call | tf_op jit(solution)/shard_map/pallas_call | solution.py:405
  59.0 30.5 %all_to_all.5 = f32[32,64,128]{2,1,0:T(8,128)S(1)} all-to-all(f32[32,64,128]{2,1,0:T(8,128)S(1)} %shard_map.115), channel_id=1, replica_groups=mesh['grp'=4,'dev'=8] {'dev','grp'}, dimensions={0} | all-to-all | bytes 2097152 | tf_op jit(solution)/shard_map/all_to_all | solution.py:449
  89.5 1.2 %shard_map.116 = f32[2048,128]{1,0:T(8,128)} custom-call(f32[2048,128]{1,0:T(8,128)S(1)} %bitcast.46), custom_call_target="tpu_custom_call" | custom-call | tf_op jit(solution)/shard_map/pallas_call | solution.py:220
  (55 shorter events, 4.6 us)
Async XLA Ops:
  1.1 13.2 %collective-permute-start = (f32[192,128]{1,0:T(8,128)S(1)}, f32[192,128]{1,0:T(8,128)S(1)}, u32[]{:S(2)}, u32[]{:S(2)}) collective-permute-start(f32[192,128]{1,0:T(8,128)S(1)} %bitcast.54), channel_id=1, source_target_pairs={{0,16},{1,17},{2,18},{3,19},{4,20},{5,21},{6,22},{7,23},{8,24},{9,... | collective-permute-start | bytes 294920 | tf_op jit(solution)/shard_map/ppermute | solution.py:318
  5.2 9.1 %collective-permute-start.1 = (f32[192,128]{1,0:T(8,128)S(1)}, f32[192,128]{1,0:T(8,128)S(1)}, u32[]{:S(2)}, u32[]{:S(2)}) collective-permute-start(f32[192,128]{1,0:T(8,128)S(1)} %bitcast.53), channel_id=1, source_target_pairs={{0,24},{1,25},{2,26},{3,27},{4,28},{5,29},{6,30},{7,31},{8,16},{9,... | collective-permute-start | bytes 294920 | tf_op jit(solution)/shard_map/ppermute | solution.py:318
  6.6 7.7 %collective-permute-start.2 = (f32[192,128]{1,0:T(8,128)S(1)}, f32[192,128]{1,0:T(8,128)S(1)}, u32[]{:S(2)}, u32[]{:S(2)}) collective-permute-start(f32[192,128]{1,0:T(8,128)S(1)} %bitcast.52), channel_id=1, source_target_pairs={{0,8},{1,9},{2,10},{3,11},{4,12},{5,13},{6,14},{7,15},{8,0},{9,1},... | collective-permute-start | bytes 294920 | tf_op jit(solution)/shard_map/ppermute | solution.py:318
  8.1 17.7 %collective-permute-start.6 = (f32[320,128]{1,0:T(8,128)S(1)}, f32[320,128]{1,0:T(8,128)S(1)}, u32[]{:S(2)}, u32[]{:S(2)}) collective-permute-start(f32[320,128]{1,0:T(8,128)S(1)} %bitcast.51), channel_id=1, source_target_pairs={{0,16},{1,17},{2,18},{3,19},{4,20},{5,21},{6,22},{7,23},{8,24},{9,... | collective-permute-start | bytes 491528 | tf_op jit(solution)/shard_map/ppermute | solution.py:318
  11.0 17.4 %collective-permute-start.14 = (f32[320,128]{1,0:T(8,128)S(1)}, f32[320,128]{1,0:T(8,128)S(1)}, u32[]{:S(2)}, u32[]{:S(2)}) collective-permute-start(f32[320,128]{1,0:T(8,128)S(1)} %bitcast.50), channel_id=1, source_target_pairs={{0,24},{1,25},{2,26},{3,27},{4,28},{5,29},{6,30},{7,31},{8,16},{9,... | collective-permute-start | bytes 491528 | tf_op jit(solution)/shard_map/ppermute | solution.py:318
  14.3 14.1 %collective-permute-start.15 = (f32[320,128]{1,0:T(8,128)S(1)}, f32[320,128]{1,0:T(8,128)S(1)}, u32[]{:S(2)}, u32[]{:S(2)}) collective-permute-start(f32[320,128]{1,0:T(8,128)S(1)} %bitcast.49), channel_id=1, source_target_pairs={{0,8},{1,9},{2,10},{3,11},{4,12},{5,13},{6,14},{7,15},{8,0},{9,1},... | collective-permute-start | bytes 491528 | tf_op jit(solution)/shard_map/ppermute | solution.py:318
  14.5 16.2 %collective-permute-start.3 = (f32[192,128]{1,0:T(8,128)S(1)}, f32[192,128]{1,0:T(8,128)S(1)}, u32[]{:S(2)}, u32[]{:S(2)}) collective-permute-start(f32[192,128]{1,0:T(8,128)S(1)} %get-tuple-element.38), channel_id=1, source_target_pairs={{0,2},{1,3},{2,0},{3,1},{4,6},{5,7},{6,4},{7,5},{8,10},{9,11},{10,... | collective-permute-start | bytes 294920 | tf_op jit(solution)/shard_map/ppermute | solution.py:318
  16.5 15.7 %collective-permute-start.4 = (f32[192,128]{1,0:T(8,128)S(1)}, f32[192,128]{1,0:T(8,128)S(1)}, u32[]{:S(2)}, u32[]{:S(2)}) collective-permute-start(f32[192,128]{1,0:T(8,128)S(1)} %get-tuple-element.39), channel_id=1, source_target_pairs={{0,4},{1,5},{2,6},{3,7},{4,0},{5,1},{6,2},{7,3},{8,12},{9,13},{10,... | collective-permute-start | bytes 294920 | tf_op jit(solution)/shard_map/ppermute | solution.py:318
  25.7 6.5 %collective-permute-start.5 = (f32[192,128]{1,0:T(8,128)S(1)}, f32[192,128]{1,0:T(8,128)S(1)}, u32[]{:S(2)}, u32[]{:S(2)}) collective-permute-start(f32[192,128]{1,0:T(8,128)S(1)} %get-tuple-element.40), channel_id=1, source_target_pairs={{0,6},{1,7},{2,4},{3,5},{4,2},{5,3},{6,0},{7,1},{8,14},{9,15},{10,... | collective-permute-start | bytes 294920 | tf_op jit(solution)/shard_map/ppermute | solution.py:318
  28.7 8.6 %collective-permute-start.16 = (f32[320,128]{1,0:T(8,128)S(1)}, f32[320,128]{1,0:T(8,128)S(1)}, u32[]{:S(2)}, u32[]{:S(2)}) collective-permute-start(f32[320,128]{1,0:T(8,128)S(1)} %get-tuple-element.54), channel_id=1, source_target_pairs={{0,4},{1,5},{2,6},{3,7},{4,0},{5,1},{6,2},{7,3},{8,12},{9,13},{10,... | collective-permute-start | bytes 491528 | tf_op jit(solution)/shard_map/ppermute | solution.py:318
  29.3 10.0 %collective-permute-start.17 = (f32[320,128]{1,0:T(8,128)S(1)}, f32[320,128]{1,0:T(8,128)S(1)}, u32[]{:S(2)}, u32[]{:S(2)}) collective-permute-start(f32[320,128]{1,0:T(8,128)S(1)} %get-tuple-element.55), channel_id=1, source_target_pairs={{0,6},{1,7},{2,4},{3,5},{4,2},{5,3},{6,0},{7,1},{8,14},{9,15},{10,... | collective-permute-start | bytes 491528 | tf_op jit(solution)/shard_map/ppermute | solution.py:318
  30.8 8.5 %collective-permute-start.18 = (f32[320,128]{1,0:T(8,128)S(1)}, f32[320,128]{1,0:T(8,128)S(1)}, u32[]{:S(2)}, u32[]{:S(2)}) collective-permute-start(f32[320,128]{1,0:T(8,128)S(1)} %get-tuple-element.56), channel_id=1, source_target_pairs={{0,2},{1,3},{2,0},{3,1},{4,6},{5,7},{6,4},{7,5},{8,10},{9,11},{10,... | collective-permute-start | bytes 491528 | tf_op jit(solution)/shard_map/ppermute | solution.py:318
  32.5 10.7 %collective-permute-start.7 = (f32[192,128]{1,0:T(8,128)S(1)}, f32[192,128]{1,0:T(8,128)S(1)}, u32[]{:S(2)}, u32[]{:S(2)}) collective-permute-start(f32[192,128]{1,0:T(8,128)S(1)} %get-tuple-element.47), channel_id=1, source_target_pairs={{0,16},{1,17},{2,18},{3,19},{4,20},{5,21},{6,22},{7,23},{8,24},{9,... | collective-permute-start | bytes 294920 | tf_op jit(solution)/shard_map/ppermute | solution.py:318
  35.3 8.3 %collective-permute-start.8 = (f32[192,128]{1,0:T(8,128)S(1)}, f32[192,128]{1,0:T(8,128)S(1)}, u32[]{:S(2)}, u32[]{:S(2)}) collective-permute-start(f32[192,128]{1,0:T(8,128)S(1)} %get-tuple-element.48), channel_id=1, source_target_pairs={{0,24},{1,25},{2,26},{3,27},{4,28},{5,29},{6,30},{7,31},{8,16},{9,... | collective-permute-start | bytes 294920 | tf_op jit(solution)/shard_map/ppermute | solution.py:318
  37.3 6.5 %collective-permute-start.9 = (f32[192,128]{1,0:T(8,128)S(1)}, f32[192,128]{1,0:T(8,128)S(1)}, u32[]{:S(2)}, u32[]{:S(2)}) collective-permute-start(f32[192,128]{1,0:T(8,128)S(1)} %get-tuple-element.49), channel_id=1, source_target_pairs={{0,8},{1,9},{2,10},{3,11},{4,12},{5,13},{6,14},{7,15},{8,0},{9,1},... | collective-permute-start | bytes 294920 | tf_op jit(solution)/shard_map/ppermute | solution.py:318
  39.5 15.5 %collective-permute-start.19 = (f32[320,128]{1,0:T(8,128)S(1)}, f32[320,128]{1,0:T(8,128)S(1)}, u32[]{:S(2)}, u32[]{:S(2)}) collective-permute-start(f32[320,128]{1,0:T(8,128)S(1)} %get-tuple-element.58), channel_id=1, source_target_pairs={{0,16},{1,17},{2,18},{3,19},{4,20},{5,21},{6,22},{7,23},{8,24},{9,... | collective-permute-start | bytes 491528 | tf_op jit(solution)/shard_map/ppermute | solution.py:318
  42.7 12.3 %collective-permute-start.20 = (f32[320,128]{1,0:T(8,128)S(1)}, f32[320,128]{1,0:T(8,128)S(1)}, u32[]{:S(2)}, u32[]{:S(2)}) collective-permute-start(f32[320,128]{1,0:T(8,128)S(1)} %get-tuple-element.59), channel_id=1, source_target_pairs={{0,24},{1,25},{2,26},{3,27},{4,28},{5,29},{6,30},{7,31},{8,16},{9,... | collective-permute-start | bytes 491528 | tf_op jit(solution)/shard_map/ppermute | solution.py:318
  43.2 12.4 %collective-permute-start.21 = (f32[320,128]{1,0:T(8,128)S(1)}, f32[320,128]{1,0:T(8,128)S(1)}, u32[]{:S(2)}, u32[]{:S(2)}) collective-permute-start(f32[320,128]{1,0:T(8,128)S(1)} %get-tuple-element.60), channel_id=1, source_target_pairs={{0,8},{1,9},{2,10},{3,11},{4,12},{5,13},{6,14},{7,15},{8,0},{9,1},... | collective-permute-start | bytes 491528 | tf_op jit(solution)/shard_map/ppermute | solution.py:318
  44.8 10.8 %collective-permute-start.12 = (f32[192,128]{1,0:T(8,128)S(1)}, f32[192,128]{1,0:T(8,128)S(1)}, u32[]{:S(2)}, u32[]{:S(2)}) collective-permute-start(f32[192,128]{1,0:T(8,128)S(1)} %collective-permute-done.8.refs_2_), channel_id=1, source_target_pairs={{0,1},{1,0},{2,3},{3,2},{4,5},{5,4},{6,7},{7,6},{8,9},{9,8},{10,11... | collective-permute-start | bytes 294920 | tf_op jit(solution)/shard_map/ppermute | solution.py:318
  45.0 12.1 %collective-permute-start.22 = (f32[320,128]{1,0:T(8,128)S(1)}, f32[320,128]{1,0:T(8,128)S(1)}, u32[]{:S(2)}, u32[]{:S(2)}) collective-permute-start(f32[320,128]{1,0:T(8,128)S(1)} %get-tuple-element.57.refs_8_), channel_id=1, source_target_pairs={{0,1},{1,0},{2,3},{3,2},{4,5},{5,4},{6,7},{7,6},{8,9},{9,8},{10,11... | collective-permute-start | bytes 491528 | tf_op jit(solution)/shard_map/ppermute | solution.py:318
  55.0 2.1 %collective-permute-start.23 = (f32[320,128]{1,0:T(8,128)S(1)}, f32[320,128]{1,0:T(8,128)S(1)}, u32[]{:S(2)}, u32[]{:S(2)}) collective-permute-start(f32[320,128]{1,0:T(8,128)S(1)} %collective-permute-done.19.refs_9_), channel_id=1, source_target_pairs={{0,1},{1,0},{2,3},{3,2},{4,5},{5,4},{6,7},{7,6},{8,9},{9,8},{10,11... | collective-permute-start | bytes 491528 | tf_op jit(solution)/shard_map/ppermute | solution.py:318
  55.0 2.1 %collective-permute-start.24 = (f32[320,128]{1,0:T(8,128)S(1)}, f32[320,128]{1,0:T(8,128)S(1)}, u32[]{:S(2)}, u32[]{:S(2)}) collective-permute-start(f32[320,128]{1,0:T(8,128)S(1)} %collective-permute-done.20.refs_10_), channel_id=1, source_target_pairs={{0,1},{1,0},{2,3},{3,2},{4,5},{5,4},{6,7},{7,6},{8,9},{9,8},{10,11... | collective-permute-start | bytes 491528 | tf_op jit(solution)/shard_map/ppermute | solution.py:318
  55.6 1.6 %collective-permute-start.25 = (f32[320,128]{1,0:T(8,128)S(1)}, f32[320,128]{1,0:T(8,128)S(1)}, u32[]{:S(2)}, u32[]{:S(2)}) collective-permute-start(f32[320,128]{1,0:T(8,128)S(1)} %collective-permute-done.21.refs_11_), channel_id=1, source_target_pairs={{0,1},{1,0},{2,3},{3,2},{4,5},{5,4},{6,7},{7,6},{8,9},{9,8},{10,11... | collective-permute-start | bytes 491528 | tf_op jit(solution)/shard_map/ppermute | solution.py:318
  55.6 1.5 %collective-permute-start.13 = (f32[192,128]{1,0:T(8,128)S(1)}, f32[192,128]{1,0:T(8,128)S(1)}, u32[]{:S(2)}, u32[]{:S(2)}) collective-permute-start(f32[192,128]{1,0:T(8,128)S(1)} %collective-permute-done.9.refs_3_), channel_id=1, source_target_pairs={{0,1},{1,0},{2,3},{3,2},{4,5},{5,4},{6,7},{7,6},{8,9},{9,8},{10,11... | collective-permute-start | bytes 294920 | tf_op jit(solution)/shard_map/ppermute | solution.py:318
  (11 other events, 336.4 us)

commit v3 on v2

--- a/solution.py
+++ b/solution.py
@@ -415,7 +415,7 @@
     )(rows_of(bits), near, mid, turn, fh, fl, *arrived)
 
 
-CHUNKS = (96, 160)
+CHUNKS = (128, 128)
 
 
 def after(arrays, result):
@@ -429,6 +429,7 @@
     one, two = [quarters(series, start * LANES, rows * LANES) for start, rows in zip(starts, CHUNKS)]
     one = swap(one, 3)
     two = swap(two, 3)
+    one = after(one, two[1])
     one = mix(one, (True,), tables[0][0])
     one = swap(one, 1)
     one = after(one, two[2])
@@ -439,6 +440,7 @@
     two = mix(two, (False,) * (CHUNKS[1] // 32), tables[1][1])
     two = swap(two, 3)
     arrived = []
+    one = after(one[:2], one[2]) + one[2:]
     for parts in (one, two):
         mine = [parts[m] for m in FAR_FIRST]
         arrived += mine + [send(part, 1) for part in mine]

time: 92 us -> 91.7 us (level)
  starting transfers between devices: 30.6 us -> 36.4 us
  waiting for transfers between devices: 23 us -> 18.1 us
  blocking collectives: 30.5 us -> 29.4 us
    ppermute x26, starting transfers between devices: 30.6 us -> 36.4 us  [send(): lax.ppermute(part, AXES, [(d, d ^ flip) for d in range(lax.axis_size(AXES...]
    ppermute x26, waiting for transfers between devices: 23 us -> 18.1 us  [send(): lax.ppermute(part, AXES, [(d, d ^ flip) for d in range(lax.axis_size(AXES...]
    all_to_all x1, blocking collectives: 30.5 us -> 29.4 us  [by_axes(): lax.all_to_all(spectrum, ORDER, split_axis=0, concat_axis=0, tiled=True)]
  transfers between devices with their start and end apart: 26 -> 26, of which waited for: 7 -> 9; matrix products, arithmetic and copies ran while one was open for 0% -> 0% of each run, Pallas kernels for 2% -> 2%
where the time goes in v3:
time: 91.7 us; the launch traced here: 90.4 us
  starting transfers between devices  36.4 us (40%)
  blocking collectives  29.4 us (32%)
  waiting for transfers between devices  18.1 us (20%)
  Pallas kernels  6.36 us (7%)
    ppermute x26, starting transfers between devices, send(): lax.ppermute(part, AXES, [(d, d ^ flip) for d in range(lax.axis_size(AXES...  36.4 us
    all_to_all x1, blocking collectives, by_axes(): lax.all_to_all(spectrum, ORDER, split_axis=0, concat_axis=0, tiled=True)  29.4 us
    ppermute x26, waiting for transfers between devices, send(): lax.ppermute(part, AXES, [(d, d ^ flip) for d in range(lax.axis_size(AXES...  18.1 us
    pallas_call x2, Pallas kernels, quarters(): pl.pallas_call(functools.partial(quarter_kernel, start), in_specs=[pl.Blo...  2.4 us
    pallas_call x1, Pallas kernels, slab_transform(): pl.pallas_call(functools.partial(slab_kernel, starts), in_specs=[VMEM_WHO...  1.83 us
  transfers between devices with their start and end apart: 26, of which 9 were waited for; matrix products, arithmetic and copies ran while one was open for 0% of the time, Pallas kernels for 2%

profile of v3, /device:TPU:0, one launch (start us, length us, event | category | flops | bytes accessed | tf_op | source)
XLA Modules:
  0.0 90.4 jit_solution(10278111840561013)
XLA Ops:
  0.0 1.2 %shard_map.110 = (f32[2,16384]{1,0:T(2,128)S(1)}, f32[2,16384]{1,0:T(2,128)S(1)}, f32[2,16384]{1,0:T(2,128)S(1)}, f32[2,16384]{1,0:T(2,128)S(1)}) custom-call(f32[2,131072]{1,0:T(2,128)} %in_ref.3), custom_call_target="tpu_custom_call" | custom-call | tf_op jit(solution)/shard_map/pallas_call | solution.py:302
  1.2 4.1 %collective-permute-start.7 = (f32[256,128]{1,0:T(8,128)S(1)}, f32[256,128]{1,0:T(8,128)S(1)}, u32[]{:S(2)}, u32[]{:S(2)}) collective-permute-start(f32[256,128]{1,0:T(8,128)S(1)} %bitcast.54), channel_id=1, source_target_pairs={{0,16},{1,17},{2,18},{3,19},{4,20},{5,21},{6,22},{7,23},{8,24},{9,... | collective-permute-start | bytes 393224 | tf_op jit(solution)/shard_map/ppermute | solution.py:318
  5.3 1.6 %collective-permute-start.3 = (f32[256,128]{1,0:T(8,128)S(1)}, f32[256,128]{1,0:T(8,128)S(1)}, u32[]{:S(2)}, u32[]{:S(2)}) collective-permute-start(f32[256,128]{1,0:T(8,128)S(1)} %bitcast.53), channel_id=1, source_target_pairs={{0,8},{1,9},{2,10},{3,11},{4,12},{5,13},{6,14},{7,15},{8,0},{9,1},... | collective-permute-start | bytes 393224 | tf_op jit(solution)/shard_map/ppermute | solution.py:318
  6.9 1.2 %shard_map.109 = (f32[2,16384]{1,0:T(2,128)S(1)}, f32[2,16384]{1,0:T(2,128)S(1)}, f32[2,16384]{1,0:T(2,128)S(1)}, f32[2,16384]{1,0:T(2,128)S(1)}) custom-call(f32[2,131072]{1,0:T(2,128)} %in_ref.3), custom_call_target="tpu_custom_call" | custom-call | tf_op jit(solution)/shard_map/pallas_call | solution.py:302
  8.1 0.9 %collective-permute-start = (f32[256,128]{1,0:T(8,128)S(1)}, f32[256,128]{1,0:T(8,128)S(1)}, u32[]{:S(2)}, u32[]{:S(2)}) collective-permute-start(f32[256,128]{1,0:T(8,128)S(1)} %bitcast.51), channel_id=1, source_target_pairs={{0,8},{1,9},{2,10},{3,11},{4,12},{5,13},{6,14},{7,15},{8,0},{9,1},... | collective-permute-start | bytes 393224 | tf_op jit(solution)/shard_map/ppermute | solution.py:318
  9.1 3.5 %collective-permute-start.1 = (f32[256,128]{1,0:T(8,128)S(1)}, f32[256,128]{1,0:T(8,128)S(1)}, u32[]{:S(2)}, u32[]{:S(2)}) collective-permute-start(f32[256,128]{1,0:T(8,128)S(1)} %bitcast.50), channel_id=1, source_target_pairs={{0,16},{1,17},{2,18},{3,19},{4,20},{5,21},{6,22},{7,23},{8,24},{9,... | collective-permute-start | bytes 393224 | tf_op jit(solution)/shard_map/ppermute | solution.py:318
  12.5 0.7 collective-permute-done.7.refs_1_
  13.2 3.8 %collective-permute-start.2 = (f32[256,128]{1,0:T(8,128)S(1)}, f32[256,128]{1,0:T(8,128)S(1)}, u32[]{:S(2)}, u32[]{:S(2)}) collective-permute-start(f32[256,128]{1,0:T(8,128)S(1)} %bitcast.49), channel_id=1, source_target_pairs={{0,24},{1,25},{2,26},{3,27},{4,28},{5,29},{6,30},{7,31},{8,16},{9,... | collective-permute-start | bytes 393224 | tf_op jit(solution)/shard_map/ppermute | solution.py:318
  17.3 1.6 %collective-permute-start.16 = (f32[256,128]{1,0:T(8,128)S(1)}, f32[256,128]{1,0:T(8,128)S(1)}, u32[]{:S(2)}, u32[]{:S(2)}) collective-permute-start(f32[256,128]{1,0:T(8,128)S(1)} %get-tuple-element.66), channel_id=1, source_target_pairs={{0,4},{1,5},{2,6},{3,7},{4,0},{5,1},{6,2},{7,3},{8,12},{9,13},{10,... | collective-permute-start | bytes 393224 | tf_op jit(solution)/shard_map/ppermute | solution.py:318
  18.9 1.4 %collective-permute-start.17 = (f32[256,128]{1,0:T(8,128)S(1)}, f32[256,128]{1,0:T(8,128)S(1)}, u32[]{:S(2)}, u32[]{:S(2)}) collective-permute-start(f32[256,128]{1,0:T(8,128)S(1)} %get-tuple-element.67), channel_id=1, source_target_pairs={{0,6},{1,7},{2,4},{3,5},{4,2},{5,3},{6,0},{7,1},{8,14},{9,15},{10,... | collective-permute-start | bytes 393224 | tf_op jit(solution)/shard_map/ppermute | solution.py:318
  20.4 0.5 collective-permute-start.18
  20.9 5.6 %collective-permute-done.1.refs_1_ = f32[256,128]{1,0:T(8,128)S(1)} collective-permute-done((f32[256,128]{1,0:T(8,128)S(1)}, f32[256,128]{1,0:T(8,128)S(1)}, u32[]{:S(2)}, u32[]{:S(2)}) %collective-permute-start.1) | collective-permute-done | bytes 131104 | tf_op jit(solution)/shard_map/ppermute | solution.py:318
  26.7 1.9 %collective-permute-start.4 = (f32[256,128]{1,0:T(8,128)S(1)}, f32[256,128]{1,0:T(8,128)S(1)}, u32[]{:S(2)}, u32[]{:S(2)}) collective-permute-start(f32[256,128]{1,0:T(8,128)S(1)} %get-tuple-element.49), channel_id=1, source_target_pairs={{0,2},{1,3},{2,0},{3,1},{4,6},{5,7},{6,4},{7,5},{8,10},{9,11},{10,... | collective-permute-start | bytes 393224 | tf_op jit(solution)/shard_map/ppermute | solution.py:318
  28.6 1.5 %collective-permute-start.5 = (f32[256,128]{1,0:T(8,128)S(1)}, f32[256,128]{1,0:T(8,128)S(1)}, u32[]{:S(2)}, u32[]{:S(2)}) collective-permute-start(f32[256,128]{1,0:T(8,128)S(1)} %get-tuple-element.50), channel_id=1, source_target_pairs={{0,4},{1,5},{2,6},{3,7},{4,0},{5,1},{6,2},{7,3},{8,12},{9,13},{10,... | collective-permute-start | bytes 393224 | tf_op jit(solution)/shard_map/ppermute | solution.py:318
  30.5 4.7 %collective-permute-start.19 = (f32[256,128]{1,0:T(8,128)S(1)}, f32[256,128]{1,0:T(8,128)S(1)}, u32[]{:S(2)}, u32[]{:S(2)}) collective-permute-start(f32[256,128]{1,0:T(8,128)S(1)} %get-tuple-element.70), channel_id=1, source_target_pairs={{0,16},{1,17},{2,18},{3,19},{4,20},{5,21},{6,22},{7,23},{8,24},{9,... | collective-permute-start | bytes 393224 | tf_op jit(solution)/shard_map/ppermute | solution.py:318
  36.2 3.0 %collective-permute-start.8 = (f32[256,128]{1,0:T(8,128)S(1)}, f32[256,128]{1,0:T(8,128)S(1)}, u32[]{:S(2)}, u32[]{:S(2)}) collective-permute-start(f32[256,128]{1,0:T(8,128)S(1)} %get-tuple-element.58), channel_id=1, source_target_pairs={{0,8},{1,9},{2,10},{3,11},{4,12},{5,13},{6,14},{7,15},{8,0},{9,1},... | collective-permute-start | bytes 393224 | tf_op jit(solution)/shard_map/ppermute | solution.py:318
  39.3 2.0 %collective-permute-start.9 = (f32[256,128]{1,0:T(8,128)S(1)}, f32[256,128]{1,0:T(8,128)S(1)}, u32[]{:S(2)}, u32[]{:S(2)}) collective-permute-start(f32[256,128]{1,0:T(8,128)S(1)} %get-tuple-element.59), channel_id=1, source_target_pairs={{0,16},{1,17},{2,18},{3,19},{4,20},{5,21},{6,22},{7,23},{8,24},{9,... | collective-permute-start | bytes 393224 | tf_op jit(solution)/shard_map/ppermute | solution.py:318
  41.3 1.9 %collective-permute-start.21 = (f32[256,128]{1,0:T(8,128)S(1)}, f32[256,128]{1,0:T(8,128)S(1)}, u32[]{:S(2)}, u32[]{:S(2)}) collective-permute-start(f32[256,128]{1,0:T(8,128)S(1)} %get-tuple-element.72), channel_id=1, source_target_pairs={{0,8},{1,9},{2,10},{3,11},{4,12},{5,13},{6,14},{7,15},{8,0},{9,1},... | collective-permute-start | bytes 393224 | tf_op jit(solution)/shard_map/ppermute | solution.py:318
  43.2 2.1 %collective-permute-done.19.refs_9_ = f32[256,128]{1,0:T(8,128)S(1)} collective-permute-done((f32[256,128]{1,0:T(8,128)S(1)}, f32[256,128]{1,0:T(8,128)S(1)}, u32[]{:S(2)}, u32[]{:S(2)}) %collective-permute-start.19) | collective-permute-done | bytes 131104 | tf_op jit(solution)/shard_map/ppermute | solution.py:318
  45.3 1.7 %collective-permute-start.10 = (f32[256,128]{1,0:T(8,128)S(1)}, f32[256,128]{1,0:T(8,128)S(1)}, u32[]{:S(2)}, u32[]{:S(2)}) collective-permute-start(f32[256,128]{1,0:T(8,128)S(1)} %get-tuple-element.61), channel_id=1, source_target_pairs={{0,24},{1,25},{2,26},{3,27},{4,28},{5,29},{6,30},{7,31},{8,16},{9,... | collective-permute-start | bytes 393224 | tf_op jit(solution)/shard_map/ppermute | solution.py:318
  47.2 8.0 %collective-permute-done.9.refs_1_ = f32[256,128]{1,0:T(8,128)S(1)} collective-permute-done((f32[256,128]{1,0:T(8,128)S(1)}, f32[256,128]{1,0:T(8,128)S(1)}, u32[]{:S(2)}, u32[]{:S(2)}) %collective-permute-start.9) | collective-permute-done | bytes 131104 | tf_op jit(solution)/shard_map/ppermute | solution.py:318
  58.0 1.8 %shard_map.115 = f32[32,64,128]{2,1,0:T(8,128)S(1)} custom-call(f32[32,128]{1,0:T(8,128)S(1)} %copy-done.6, f32[2048,128]{1,0:T(8,128)S(1)} %copy-done.2, f32[2048,128]{1,0:T(8,128)S(1)} %copy-done.1, f32[2048,128]{1,0:T(8,128)S(1)} %copy-done, bf16[256,256]{1,0:T(8,128)(2,1)S(1)} %copy-done.4, bf16[256,256]{1,0:T(8,128)(2,1)S(1)} %copy-done.3, ...), custom_call_target="tpu_custom_call" | custom-call | tf_op jit(solution)/shard_map/pallas_call | solution.py:405
  59.8 29.4 %all_to_all.5 = f32[32,64,128]{2,1,0:T(8,128)S(1)} all-to-all(f32[32,64,128]{2,1,0:T(8,128)S(1)} %shard_map.115), channel_id=1, replica_groups=mesh['grp'=4,'dev'=8] {'dev','grp'}, dimensions={0} | all-to-all | bytes 2097152 | tf_op jit(solution)/shard_map/all_to_all | solution.py:451
  89.2 1.2 %shard_map.116 = f32[2048,128]{1,0:T(8,128)} custom-call(f32[2048,128]{1,0:T(8,128)S(1)} %bitcast.46), custom_call_target="tpu_custom_call" | custom-call | tf_op jit(solution)/shard_map/pallas_call | solution.py:220
  (55 shorter events, 4.8 us)
Async XLA Ops:
  1.2 12.1 %collective-permute-start.7 = (f32[256,128]{1,0:T(8,128)S(1)}, f32[256,128]{1,0:T(8,128)S(1)}, u32[]{:S(2)}, u32[]{:S(2)}) collective-permute-start(f32[256,128]{1,0:T(8,128)S(1)} %bitcast.54), channel_id=1, source_target_pairs={{0,16},{1,17},{2,18},{3,19},{4,20},{5,21},{6,22},{7,23},{8,24},{9,... | collective-permute-start | bytes 393224 | tf_op jit(solution)/shard_map/ppermute | solution.py:318
  5.3 11.8 %collective-permute-start.3 = (f32[256,128]{1,0:T(8,128)S(1)}, f32[256,128]{1,0:T(8,128)S(1)}, u32[]{:S(2)}, u32[]{:S(2)}) collective-permute-start(f32[256,128]{1,0:T(8,128)S(1)} %bitcast.53), channel_id=1, source_target_pairs={{0,8},{1,9},{2,10},{3,11},{4,12},{5,13},{6,14},{7,15},{8,0},{9,1},... | collective-permute-start | bytes 393224 | tf_op jit(solution)/shard_map/ppermute | solution.py:318
  6.9 10.2 %collective-permute-start.15 = (f32[256,128]{1,0:T(8,128)S(1)}, f32[256,128]{1,0:T(8,128)S(1)}, u32[]{:S(2)}, u32[]{:S(2)}) collective-permute-start(f32[256,128]{1,0:T(8,128)S(1)} %bitcast.52), channel_id=1, source_target_pairs={{0,24},{1,25},{2,26},{3,27},{4,28},{5,29},{6,30},{7,31},{8,16},{9,... | collective-permute-start | bytes 393224 | tf_op jit(solution)/shard_map/ppermute | solution.py:318
  8.1 12.2 %collective-permute-start = (f32[256,128]{1,0:T(8,128)S(1)}, f32[256,128]{1,0:T(8,128)S(1)}, u32[]{:S(2)}, u32[]{:S(2)}) collective-permute-start(f32[256,128]{1,0:T(8,128)S(1)} %bitcast.51), channel_id=1, source_target_pairs={{0,8},{1,9},{2,10},{3,11},{4,12},{5,13},{6,14},{7,15},{8,0},{9,1},... | collective-permute-start | bytes 393224 | tf_op jit(solution)/shard_map/ppermute | solution.py:318
  9.1 17.4 %collective-permute-start.1 = (f32[256,128]{1,0:T(8,128)S(1)}, f32[256,128]{1,0:T(8,128)S(1)}, u32[]{:S(2)}, u32[]{:S(2)}) collective-permute-start(f32[256,128]{1,0:T(8,128)S(1)} %bitcast.50), channel_id=1, source_target_pairs={{0,16},{1,17},{2,18},{3,19},{4,20},{5,21},{6,22},{7,23},{8,24},{9,... | collective-permute-start | bytes 393224 | tf_op jit(solution)/shard_map/ppermute | solution.py:318
  13.2 13.2 %collective-permute-start.2 = (f32[256,128]{1,0:T(8,128)S(1)}, f32[256,128]{1,0:T(8,128)S(1)}, u32[]{:S(2)}, u32[]{:S(2)}) collective-permute-start(f32[256,128]{1,0:T(8,128)S(1)} %bitcast.49), channel_id=1, source_target_pairs={{0,24},{1,25},{2,26},{3,27},{4,28},{5,29},{6,30},{7,31},{8,16},{9,... | collective-permute-start | bytes 393224 | tf_op jit(solution)/shard_map/ppermute | solution.py:318
  17.3 12.8 %collective-permute-start.16 = (f32[256,128]{1,0:T(8,128)S(1)}, f32[256,128]{1,0:T(8,128)S(1)}, u32[]{:S(2)}, u32[]{:S(2)}) collective-permute-start(f32[256,128]{1,0:T(8,128)S(1)} %get-tuple-element.66), channel_id=1, source_target_pairs={{0,4},{1,5},{2,6},{3,7},{4,0},{5,1},{6,2},{7,3},{8,12},{9,13},{10,... | collective-permute-start | bytes 393224 | tf_op jit(solution)/shard_map/ppermute | solution.py:318
  18.9 11.3 %collective-permute-start.17 = (f32[256,128]{1,0:T(8,128)S(1)}, f32[256,128]{1,0:T(8,128)S(1)}, u32[]{:S(2)}, u32[]{:S(2)}) collective-permute-start(f32[256,128]{1,0:T(8,128)S(1)} %get-tuple-element.67), channel_id=1, source_target_pairs={{0,6},{1,7},{2,4},{3,5},{4,2},{5,3},{6,0},{7,1},{8,14},{9,15},{10,... | collective-permute-start | bytes 393224 | tf_op jit(solution)/shard_map/ppermute | solution.py:318
  20.4 9.9 %collective-permute-start.18 = (f32[256,128]{1,0:T(8,128)S(1)}, f32[256,128]{1,0:T(8,128)S(1)}, u32[]{:S(2)}, u32[]{:S(2)}) collective-permute-start(f32[256,128]{1,0:T(8,128)S(1)} %get-tuple-element.68), channel_id=1, source_target_pairs={{0,2},{1,3},{2,0},{3,1},{4,6},{5,7},{6,4},{7,5},{8,10},{9,11},{10,... | collective-permute-start | bytes 393224 | tf_op jit(solution)/shard_map/ppermute | solution.py:318
  26.7 9.0 %collective-permute-start.4 = (f32[256,128]{1,0:T(8,128)S(1)}, f32[256,128]{1,0:T(8,128)S(1)}, u32[]{:S(2)}, u32[]{:S(2)}) collective-permute-start(f32[256,128]{1,0:T(8,128)S(1)} %get-tuple-element.49), channel_id=1, source_target_pairs={{0,2},{1,3},{2,0},{3,1},{4,6},{5,7},{6,4},{7,5},{8,10},{9,11},{10,... | collective-permute-start | bytes 393224 | tf_op jit(solution)/shard_map/ppermute | solution.py:318
  28.6 7.1 %collective-permute-start.5 = (f32[256,128]{1,0:T(8,128)S(1)}, f32[256,128]{1,0:T(8,128)S(1)}, u32[]{:S(2)}, u32[]{:S(2)}) collective-permute-start(f32[256,128]{1,0:T(8,128)S(1)} %get-tuple-element.50), channel_id=1, source_target_pairs={{0,4},{1,5},{2,6},{3,7},{4,0},{5,1},{6,2},{7,3},{8,12},{9,13},{10,... | collective-permute-start | bytes 393224 | tf_op jit(solution)/shard_map/ppermute | solution.py:318
  30.1 5.9 %collective-permute-start.6 = (f32[256,128]{1,0:T(8,128)S(1)}, f32[256,128]{1,0:T(8,128)S(1)}, u32[]{:S(2)}, u32[]{:S(2)}) collective-permute-start(f32[256,128]{1,0:T(8,128)S(1)} %get-tuple-element.51), channel_id=1, source_target_pairs={{0,6},{1,7},{2,4},{3,5},{4,2},{5,3},{6,0},{7,1},{8,14},{9,15},{10,... | collective-permute-start | bytes 393224 | tf_op jit(solution)/shard_map/ppermute | solution.py:318
  30.5 14.8 %collective-permute-start.19 = (f32[256,128]{1,0:T(8,128)S(1)}, f32[256,128]{1,0:T(8,128)S(1)}, u32[]{:S(2)}, u32[]{:S(2)}) collective-permute-start(f32[256,128]{1,0:T(8,128)S(1)} %get-tuple-element.70), channel_id=1, source_target_pairs={{0,16},{1,17},{2,18},{3,19},{4,20},{5,21},{6,22},{7,23},{8,24},{9,... | collective-permute-start | bytes 393224 | tf_op jit(solution)/shard_map/ppermute | solution.py:318
  35.2 10.0 %collective-permute-start.20 = (f32[256,128]{1,0:T(8,128)S(1)}, f32[256,128]{1,0:T(8,128)S(1)}, u32[]{:S(2)}, u32[]{:S(2)}) collective-permute-start(f32[256,128]{1,0:T(8,128)S(1)} %get-tuple-element.71), channel_id=1, source_target_pairs={{0,24},{1,25},{2,26},{3,27},{4,28},{5,29},{6,30},{7,31},{8,16},{9,... | collective-permute-start | bytes 393224 | tf_op jit(solution)/shard_map/ppermute | solution.py:318
  36.2 10.7 %collective-permute-start.8 = (f32[256,128]{1,0:T(8,128)S(1)}, f32[256,128]{1,0:T(8,128)S(1)}, u32[]{:S(2)}, u32[]{:S(2)}) collective-permute-start(f32[256,128]{1,0:T(8,128)S(1)} %get-tuple-element.58), channel_id=1, source_target_pairs={{0,8},{1,9},{2,10},{3,11},{4,12},{5,13},{6,14},{7,15},{8,0},{9,1},... | collective-permute-start | bytes 393224 | tf_op jit(solution)/shard_map/ppermute | solution.py:318
  39.3 16.0 %collective-permute-start.9 = (f32[256,128]{1,0:T(8,128)S(1)}, f32[256,128]{1,0:T(8,128)S(1)}, u32[]{:S(2)}, u32[]{:S(2)}) collective-permute-start(f32[256,128]{1,0:T(8,128)S(1)} %get-tuple-element.59), channel_id=1, source_target_pairs={{0,16},{1,17},{2,18},{3,19},{4,20},{5,21},{6,22},{7,23},{8,24},{9,... | collective-permute-start | bytes 393224 | tf_op jit(solution)/shard_map/ppermute | solution.py:318
  41.3 14.0 %collective-permute-start.21 = (f32[256,128]{1,0:T(8,128)S(1)}, f32[256,128]{1,0:T(8,128)S(1)}, u32[]{:S(2)}, u32[]{:S(2)}) collective-permute-start(f32[256,128]{1,0:T(8,128)S(1)} %get-tuple-element.72), channel_id=1, source_target_pairs={{0,8},{1,9},{2,10},{3,11},{4,12},{5,13},{6,14},{7,15},{8,0},{9,1},... | collective-permute-start | bytes 393224 | tf_op jit(solution)/shard_map/ppermute | solution.py:318
  45.3 10.5 %collective-permute-start.22 = (f32[256,128]{1,0:T(8,128)S(1)}, f32[256,128]{1,0:T(8,128)S(1)}, u32[]{:S(2)}, u32[]{:S(2)}) collective-permute-start(f32[256,128]{1,0:T(8,128)S(1)} %get-tuple-element.69.refs_8_), channel_id=1, source_target_pairs={{0,1},{1,0},{2,3},{3,2},{4,5},{5,4},{6,7},{7,6},{8,9},{9,8},{10,11... | collective-permute-start | bytes 393224 | tf_op jit(solution)/shard_map/ppermute | solution.py:318
  45.3 10.5 %collective-permute-start.10 = (f32[256,128]{1,0:T(8,128)S(1)}, f32[256,128]{1,0:T(8,128)S(1)}, u32[]{:S(2)}, u32[]{:S(2)}) collective-permute-start(f32[256,128]{1,0:T(8,128)S(1)} %get-tuple-element.61), channel_id=1, source_target_pairs={{0,24},{1,25},{2,26},{3,27},{4,28},{5,29},{6,30},{7,31},{8,16},{9,... | collective-permute-start | bytes 393224 | tf_op jit(solution)/shard_map/ppermute | solution.py:318
  47.0 9.3 %collective-permute-start.23 = (f32[256,128]{1,0:T(8,128)S(1)}, f32[256,128]{1,0:T(8,128)S(1)}, u32[]{:S(2)}, u32[]{:S(2)}) collective-permute-start(f32[256,128]{1,0:T(8,128)S(1)} %collective-permute-done.19.refs_9_), channel_id=1, source_target_pairs={{0,1},{1,0},{2,3},{3,2},{4,5},{5,4},{6,7},{7,6},{8,9},{9,8},{10,11... | collective-permute-start | bytes 393224 | tf_op jit(solution)/shard_map/ppermute | solution.py:318
  55.2 2.1 %collective-permute-start.11 = (f32[256,128]{1,0:T(8,128)S(1)}, f32[256,128]{1,0:T(8,128)S(1)}, u32[]{:S(2)}, u32[]{:S(2)}) collective-permute-start(f32[256,128]{1,0:T(8,128)S(1)} %get-tuple-element.60.refs_0_), channel_id=1, source_target_pairs={{0,1},{1,0},{2,3},{3,2},{4,5},{5,4},{6,7},{7,6},{8,9},{9,8},{10,11... | collective-permute-start | bytes 393224 | tf_op jit(solution)/shard_map/ppermute | solution.py:318
  55.7 1.5 %collective-permute-start.14 = (f32[256,128]{1,0:T(8,128)S(1)}, f32[256,128]{1,0:T(8,128)S(1)}, u32[]{:S(2)}, u32[]{:S(2)}) collective-permute-start(f32[256,128]{1,0:T(8,128)S(1)} %collective-permute-done.8.refs_3_), channel_id=1, source_target_pairs={{0,1},{1,0},{2,3},{3,2},{4,5},{5,4},{6,7},{7,6},{8,9},{9,8},{10,11... | collective-permute-start | bytes 393224 | tf_op jit(solution)/shard_map/ppermute | solution.py:318
  55.8 1.5 %collective-permute-start.25 = (f32[256,128]{1,0:T(8,128)S(1)}, f32[256,128]{1,0:T(8,128)S(1)}, u32[]{:S(2)}, u32[]{:S(2)}) collective-permute-start(f32[256,128]{1,0:T(8,128)S(1)} %collective-permute-done.21.refs_11_), channel_id=1, source_target_pairs={{0,1},{1,0},{2,3},{3,2},{4,5},{5,4},{6,7},{7,6},{8,9},{9,8},{10,11... | collective-permute-start | bytes 393224 | tf_op jit(solution)/shard_map/ppermute | solution.py:318
  56.3 1.3 %collective-permute-start.12 = (f32[256,128]{1,0:T(8,128)S(1)}, f32[256,128]{1,0:T(8,128)S(1)}, u32[]{:S(2)}, u32[]{:S(2)}) collective-permute-start(f32[256,128]{1,0:T(8,128)S(1)} %collective-permute-done.9.refs_1_), channel_id=1, source_target_pairs={{0,1},{1,0},{2,3},{3,2},{4,5},{5,4},{6,7},{7,6},{8,9},{9,8},{10,11... | collective-permute-start | bytes 393224 | tf_op jit(solution)/shard_map/ppermute | solution.py:318
  (11 other events, 336.1 us)

commit v4 on v3

--- a/solution.py
+++ b/solution.py
@@ -444,12 +444,11 @@
     for parts in (one, two):
         mine = [parts[m] for m in FAR_FIRST]
         arrived += mine + [send(part, 1) for part in mine]
-    at = np.arange(32).reshape(8, 4).T.reshape(-1)
-    dest, c, low = np.meshgrid(np.argsort(at), np.arange(2), np.arange(4), indexing="ij")
+    dest, c, low = np.meshgrid(np.arange(32), np.arange(2), np.arange(4), indexing="ij")
     lane_rows = ((dest * 4 + low).reshape(-1), (c == 1).reshape(-1))
     spectrum = slab_transform(arrived, lane_rows, points)
-    landed = lax.all_to_all(spectrum, ORDER, split_axis=0, concat_axis=0, tiled=True).reshape(2048, LANES)
-    ordered = order_rows(landed, at[np.argsort(device_digits()[3])].tolist())
+    landed = lax.all_to_all(spectrum, AXES, split_axis=0, concat_axis=0, tiled=True).reshape(2048, LANES)
+    ordered = order_rows(landed, np.argsort(device_digits()[3]).tolist())
     return ordered.reshape(slab // LANES, 2, LANES).transpose(1, 0, 2).reshape(2, slab)
 
 

time: 91.7 us -> 91.8 us (level); the launches traced: 90.4 us -> 91.6 us
  blocking collectives: 29.4 us -> 30.6 us
    all_to_all x1, blocking collectives: 29.4 us -> 30.6 us  [by_axes(): lax.all_to_all(spectrum, AXES, split_axis=0, concat_axis=0, tiled=True)]
where the time goes in v4:
time: 91.8 us; the launch traced here: 91.6 us
  starting transfers between devices  36.4 us (40%)
  blocking collectives  30.6 us (33%)
  waiting for transfers between devices  18.1 us (20%)
  Pallas kernels  6.36 us (7%)
    ppermute x26, starting transfers between devices, send(): lax.ppermute(part, AXES, [(d, d ^ flip) for d in range(lax.axis_size(AXES...  36.4 us
    all_to_all x1, blocking collectives, by_axes(): lax.all_to_all(spectrum, AXES, split_axis=0, concat_axis=0, tiled=True)  30.6 us
    ppermute x26, waiting for transfers between devices, send(): lax.ppermute(part, AXES, [(d, d ^ flip) for d in range(lax.axis_size(AXES...  18.1 us
    pallas_call x2, Pallas kernels, quarters(): pl.pallas_call(functools.partial(quarter_kernel, start), in_specs=[pl.Blo...  2.4 us
  transfers between devices with their start and end apart: 26, of which 9 were waited for; matrix products, arithmetic and copies ran while one was open for 0% of the time, Pallas kernels for 2%

profile of v4, /device:TPU:0, one launch (start us, length us, event | category | flops | bytes accessed | tf_op | source)
XLA Modules:
  0.0 91.6 jit_solution(15367507386148811704)
XLA Ops:
  0.0 1.2 %shard_map.110 = (f32[2,16384]{1,0:T(2,128)S(1)}, f32[2,16384]{1,0:T(2,128)S(1)}, f32[2,16384]{1,0:T(2,128)S(1)}, f32[2,16384]{1,0:T(2,128)S(1)}) custom-call(f32[2,131072]{1,0:T(2,128)} %in_ref.3), custom_call_target="tpu_custom_call" | custom-call | tf_op jit(solution)/shard_map/pallas_call | solution.py:302
  1.2 4.1 %collective-permute-start.7 = (f32[256,128]{1,0:T(8,128)S(1)}, f32[256,128]{1,0:T(8,128)S(1)}, u32[]{:S(2)}, u32[]{:S(2)}) collective-permute-start(f32[256,128]{1,0:T(8,128)S(1)} %bitcast.54), channel_id=1, source_target_pairs={{0,16},{1,17},{2,18},{3,19},{4,20},{5,21},{6,22},{7,23},{8,24},{9,... | collective-permute-start | bytes 393224 | tf_op jit(solution)/shard_map/ppermute | solution.py:318
  5.3 1.6 %collective-permute-start.3 = (f32[256,128]{1,0:T(8,128)S(1)}, f32[256,128]{1,0:T(8,128)S(1)}, u32[]{:S(2)}, u32[]{:S(2)}) collective-permute-start(f32[256,128]{1,0:T(8,128)S(1)} %bitcast.53), channel_id=1, source_target_pairs={{0,8},{1,9},{2,10},{3,11},{4,12},{5,13},{6,14},{7,15},{8,0},{9,1},... | collective-permute-start | bytes 393224 | tf_op jit(solution)/shard_map/ppermute | solution.py:318
  6.9 1.2 %shard_map.109 = (f32[2,16384]{1,0:T(2,128)S(1)}, f32[2,16384]{1,0:T(2,128)S(1)}, f32[2,16384]{1,0:T(2,128)S(1)}, f32[2,16384]{1,0:T(2,128)S(1)}) custom-call(f32[2,131072]{1,0:T(2,128)} %in_ref.3), custom_call_target="tpu_custom_call" | custom-call | tf_op jit(solution)/shard_map/pallas_call | solution.py:302
  8.1 0.9 %collective-permute-start = (f32[256,128]{1,0:T(8,128)S(1)}, f32[256,128]{1,0:T(8,128)S(1)}, u32[]{:S(2)}, u32[]{:S(2)}) collective-permute-start(f32[256,128]{1,0:T(8,128)S(1)} %bitcast.51), channel_id=1, source_target_pairs={{0,8},{1,9},{2,10},{3,11},{4,12},{5,13},{6,14},{7,15},{8,0},{9,1},... | collective-permute-start | bytes 393224 | tf_op jit(solution)/shard_map/ppermute | solution.py:318
  9.1 3.5 %collective-permute-start.1 = (f32[256,128]{1,0:T(8,128)S(1)}, f32[256,128]{1,0:T(8,128)S(1)}, u32[]{:S(2)}, u32[]{:S(2)}) collective-permute-start(f32[256,128]{1,0:T(8,128)S(1)} %bitcast.50), channel_id=1, source_target_pairs={{0,16},{1,17},{2,18},{3,19},{4,20},{5,21},{6,22},{7,23},{8,24},{9,... | collective-permute-start | bytes 393224 | tf_op jit(solution)/shard_map/ppermute | solution.py:318
  12.5 0.7 collective-permute-done.7.refs_1_
  13.2 3.8 %collective-permute-start.2 = (f32[256,128]{1,0:T(8,128)S(1)}, f32[256,128]{1,0:T(8,128)S(1)}, u32[]{:S(2)}, u32[]{:S(2)}) collective-permute-start(f32[256,128]{1,0:T(8,128)S(1)} %bitcast.49), channel_id=1, source_target_pairs={{0,24},{1,25},{2,26},{3,27},{4,28},{5,29},{6,30},{7,31},{8,16},{9,... | collective-permute-start | bytes 393224 | tf_op jit(solution)/shard_map/ppermute | solution.py:318
  17.3 1.6 %collective-permute-start.16 = (f32[256,128]{1,0:T(8,128)S(1)}, f32[256,128]{1,0:T(8,128)S(1)}, u32[]{:S(2)}, u32[]{:S(2)}) collective-permute-start(f32[256,128]{1,0:T(8,128)S(1)} %get-tuple-element.66), channel_id=1, source_target_pairs={{0,4},{1,5},{2,6},{3,7},{4,0},{5,1},{6,2},{7,3},{8,12},{9,13},{10,... | collective-permute-start | bytes 393224 | tf_op jit(solution)/shard_map/ppermute | solution.py:318
  18.9 1.4 %collective-permute-start.17 = (f32[256,128]{1,0:T(8,128)S(1)}, f32[256,128]{1,0:T(8,128)S(1)}, u32[]{:S(2)}, u32[]{:S(2)}) collective-permute-start(f32[256,128]{1,0:T(8,128)S(1)} %get-tuple-element.67), channel_id=1, source_target_pairs={{0,6},{1,7},{2,4},{3,5},{4,2},{5,3},{6,0},{7,1},{8,14},{9,15},{10,... | collective-permute-start | bytes 393224 | tf_op jit(solution)/shard_map/ppermute | solution.py:318
  20.4 0.5 collective-permute-start.18
  20.9 5.6 %collective-permute-done.1.refs_1_ = f32[256,128]{1,0:T(8,128)S(1)} collective-permute-done((f32[256,128]{1,0:T(8,128)S(1)}, f32[256,128]{1,0:T(8,128)S(1)}, u32[]{:S(2)}, u32[]{:S(2)}) %collective-permute-start.1) | collective-permute-done | bytes 131104 | tf_op jit(solution)/shard_map/ppermute | solution.py:318
  26.7 1.9 %collective-permute-start.4 = (f32[256,128]{1,0:T(8,128)S(1)}, f32[256,128]{1,0:T(8,128)S(1)}, u32[]{:S(2)}, u32[]{:S(2)}) collective-permute-start(f32[256,128]{1,0:T(8,128)S(1)} %get-tuple-element.49), channel_id=1, source_target_pairs={{0,2},{1,3},{2,0},{3,1},{4,6},{5,7},{6,4},{7,5},{8,10},{9,11},{10,... | collective-permute-start | bytes 393224 | tf_op jit(solution)/shard_map/ppermute | solution.py:318
  28.6 1.5 %collective-permute-start.5 = (f32[256,128]{1,0:T(8,128)S(1)}, f32[256,128]{1,0:T(8,128)S(1)}, u32[]{:S(2)}, u32[]{:S(2)}) collective-permute-start(f32[256,128]{1,0:T(8,128)S(1)} %get-tuple-element.50), channel_id=1, source_target_pairs={{0,4},{1,5},{2,6},{3,7},{4,0},{5,1},{6,2},{7,3},{8,12},{9,13},{10,... | collective-permute-start | bytes 393224 | tf_op jit(solution)/shard_map/ppermute | solution.py:318
  30.5 4.7 %collective-permute-start.19 = (f32[256,128]{1,0:T(8,128)S(1)}, f32[256,128]{1,0:T(8,128)S(1)}, u32[]{:S(2)}, u32[]{:S(2)}) collective-permute-start(f32[256,128]{1,0:T(8,128)S(1)} %get-tuple-element.70), channel_id=1, source_target_pairs={{0,16},{1,17},{2,18},{3,19},{4,20},{5,21},{6,22},{7,23},{8,24},{9,... | collective-permute-start | bytes 393224 | tf_op jit(solution)/shard_map/ppermute | solution.py:318
  36.2 3.0 %collective-permute-start.8 = (f32[256,128]{1,0:T(8,128)S(1)}, f32[256,128]{1,0:T(8,128)S(1)}, u32[]{:S(2)}, u32[]{:S(2)}) collective-permute-start(f32[256,128]{1,0:T(8,128)S(1)} %get-tuple-element.58), channel_id=1, source_target_pairs={{0,8},{1,9},{2,10},{3,11},{4,12},{5,13},{6,14},{7,15},{8,0},{9,1},... | collective-permute-start | bytes 393224 | tf_op jit(solution)/shard_map/ppermute | solution.py:318
  39.3 2.0 %collective-permute-start.9 = (f32[256,128]{1,0:T(8,128)S(1)}, f32[256,128]{1,0:T(8,128)S(1)}, u32[]{:S(2)}, u32[]{:S(2)}) collective-permute-start(f32[256,128]{1,0:T(8,128)S(1)} %get-tuple-element.59), channel_id=1, source_target_pairs={{0,16},{1,17},{2,18},{3,19},{4,20},{5,21},{6,22},{7,23},{8,24},{9,... | collective-permute-start | bytes 393224 | tf_op jit(solution)/shard_map/ppermute | solution.py:318
  41.3 1.9 %collective-permute-start.21 = (f32[256,128]{1,0:T(8,128)S(1)}, f32[256,128]{1,0:T(8,128)S(1)}, u32[]{:S(2)}, u32[]{:S(2)}) collective-permute-start(f32[256,128]{1,0:T(8,128)S(1)} %get-tuple-element.72), channel_id=1, source_target_pairs={{0,8},{1,9},{2,10},{3,11},{4,12},{5,13},{6,14},{7,15},{8,0},{9,1},... | collective-permute-start | bytes 393224 | tf_op jit(solution)/shard_map/ppermute | solution.py:318
  43.2 2.1 %collective-permute-done.19.refs_9_ = f32[256,128]{1,0:T(8,128)S(1)} collective-permute-done((f32[256,128]{1,0:T(8,128)S(1)}, f32[256,128]{1,0:T(8,128)S(1)}, u32[]{:S(2)}, u32[]{:S(2)}) %collective-permute-start.19) | collective-permute-done | bytes 131104 | tf_op jit(solution)/shard_map/ppermute | solution.py:318
  45.3 1.7 %collective-permute-start.10 = (f32[256,128]{1,0:T(8,128)S(1)}, f32[256,128]{1,0:T(8,128)S(1)}, u32[]{:S(2)}, u32[]{:S(2)}) collective-permute-start(f32[256,128]{1,0:T(8,128)S(1)} %get-tuple-element.61), channel_id=1, source_target_pairs={{0,24},{1,25},{2,26},{3,27},{4,28},{5,29},{6,30},{7,31},{8,16},{9,... | collective-permute-start | bytes 393224 | tf_op jit(solution)/shard_map/ppermute | solution.py:318
  47.2 8.0 %collective-permute-done.9.refs_1_ = f32[256,128]{1,0:T(8,128)S(1)} collective-permute-done((f32[256,128]{1,0:T(8,128)S(1)}, f32[256,128]{1,0:T(8,128)S(1)}, u32[]{:S(2)}, u32[]{:S(2)}) %collective-permute-start.9) | collective-permute-done | bytes 131104 | tf_op jit(solution)/shard_map/ppermute | solution.py:318
  58.0 1.8 %shard_map.115 = f32[32,64,128]{2,1,0:T(8,128)S(1)} custom-call(f32[32,128]{1,0:T(8,128)S(1)} %copy-done.6, f32[2048,128]{1,0:T(8,128)S(1)} %copy-done.2, f32[2048,128]{1,0:T(8,128)S(1)} %copy-done.1, f32[2048,128]{1,0:T(8,128)S(1)} %copy-done, bf16[256,256]{1,0:T(8,128)(2,1)S(1)} %copy-done.4, bf16[256,256]{1,0:T(8,128)(2,1)S(1)} %copy-done.3, ...), custom_call_target="tpu_custom_call" | custom-call | tf_op jit(solution)/shard_map/pallas_call | solution.py:405
  59.8 30.6 %all_to_all.5 = f32[32,64,128]{2,1,0:T(8,128)S(1)} all-to-all(f32[32,64,128]{2,1,0:T(8,128)S(1)} %shard_map.115), channel_id=1, replica_groups=mesh['grp'=4,'dev'=8] {'grp','dev'}, dimensions={0} | all-to-all | bytes 2097152 | tf_op jit(solution)/shard_map/all_to_all | solution.py:450
  90.4 1.2 %shard_map.116 = f32[2048,128]{1,0:T(8,128)} custom-call(f32[2048,128]{1,0:T(8,128)S(1)} %bitcast.46), custom_call_target="tpu_custom_call" | custom-call | tf_op jit(solution)/shard_map/pallas_call | solution.py:220
  (55 shorter events, 4.8 us)
Async XLA Ops:
  1.2 12.1 %collective-permute-start.7 = (f32[256,128]{1,0:T(8,128)S(1)}, f32[256,128]{1,0:T(8,128)S(1)}, u32[]{:S(2)}, u32[]{:S(2)}) collective-permute-start(f32[256,128]{1,0:T(8,128)S(1)} %bitcast.54), channel_id=1, source_target_pairs={{0,16},{1,17},{2,18},{3,19},{4,20},{5,21},{6,22},{7,23},{8,24},{9,... | collective-permute-start | bytes 393224 | tf_op jit(solution)/shard_map/ppermute | solution.py:318
  5.3 11.8 %collective-permute-start.3 = (f32[256,128]{1,0:T(8,128)S(1)}, f32[256,128]{1,0:T(8,128)S(1)}, u32[]{:S(2)}, u32[]{:S(2)}) collective-permute-start(f32[256,128]{1,0:T(8,128)S(1)} %bitcast.53), channel_id=1, source_target_pairs={{0,8},{1,9},{2,10},{3,11},{4,12},{5,13},{6,14},{7,15},{8,0},{9,1},... | collective-permute-start | bytes 393224 | tf_op jit(solution)/shard_map/ppermute | solution.py:318
  6.9 10.2 %collective-permute-start.15 = (f32[256,128]{1,0:T(8,128)S(1)}, f32[256,128]{1,0:T(8,128)S(1)}, u32[]{:S(2)}, u32[]{:S(2)}) collective-permute-start(f32[256,128]{1,0:T(8,128)S(1)} %bitcast.52), channel_id=1, source_target_pairs={{0,24},{1,25},{2,26},{3,27},{4,28},{5,29},{6,30},{7,31},{8,16},{9,... | collective-permute-start | bytes 393224 | tf_op jit(solution)/shard_map/ppermute | solution.py:318
  8.1 12.2 %collective-permute-start = (f32[256,128]{1,0:T(8,128)S(1)}, f32[256,128]{1,0:T(8,128)S(1)}, u32[]{:S(2)}, u32[]{:S(2)}) collective-permute-start(f32[256,128]{1,0:T(8,128)S(1)} %bitcast.51), channel_id=1, source_target_pairs={{0,8},{1,9},{2,10},{3,11},{4,12},{5,13},{6,14},{7,15},{8,0},{9,1},... | collective-permute-start | bytes 393224 | tf_op jit(solution)/shard_map/ppermute | solution.py:318
  9.1 17.4 %collective-permute-start.1 = (f32[256,128]{1,0:T(8,128)S(1)}, f32[256,128]{1,0:T(8,128)S(1)}, u32[]{:S(2)}, u32[]{:S(2)}) collective-permute-start(f32[256,128]{1,0:T(8,128)S(1)} %bitcast.50), channel_id=1, source_target_pairs={{0,16},{1,17},{2,18},{3,19},{4,20},{5,21},{6,22},{7,23},{8,24},{9,... | collective-permute-start | bytes 393224 | tf_op jit(solution)/shard_map/ppermute | solution.py:318
  13.2 13.2 %collective-permute-start.2 = (f32[256,128]{1,0:T(8,128)S(1)}, f32[256,128]{1,0:T(8,128)S(1)}, u32[]{:S(2)}, u32[]{:S(2)}) collective-permute-start(f32[256,128]{1,0:T(8,128)S(1)} %bitcast.49), channel_id=1, source_target_pairs={{0,24},{1,25},{2,26},{3,27},{4,28},{5,29},{6,30},{7,31},{8,16},{9,... | collective-permute-start | bytes 393224 | tf_op jit(solution)/shard_map/ppermute | solution.py:318
  17.3 12.8 %collective-permute-start.16 = (f32[256,128]{1,0:T(8,128)S(1)}, f32[256,128]{1,0:T(8,128)S(1)}, u32[]{:S(2)}, u32[]{:S(2)}) collective-permute-start(f32[256,128]{1,0:T(8,128)S(1)} %get-tuple-element.66), channel_id=1, source_target_pairs={{0,4},{1,5},{2,6},{3,7},{4,0},{5,1},{6,2},{7,3},{8,12},{9,13},{10,... | collective-permute-start | bytes 393224 | tf_op jit(solution)/shard_map/ppermute | solution.py:318
  18.9 11.3 %collective-permute-start.17 = (f32[256,128]{1,0:T(8,128)S(1)}, f32[256,128]{1,0:T(8,128)S(1)}, u32[]{:S(2)}, u32[]{:S(2)}) collective-permute-start(f32[256,128]{1,0:T(8,128)S(1)} %get-tuple-element.67), channel_id=1, source_target_pairs={{0,6},{1,7},{2,4},{3,5},{4,2},{5,3},{6,0},{7,1},{8,14},{9,15},{10,... | collective-permute-start | bytes 393224 | tf_op jit(solution)/shard_map/ppermute | solution.py:318
  20.4 9.9 %collective-permute-start.18 = (f32[256,128]{1,0:T(8,128)S(1)}, f32[256,128]{1,0:T(8,128)S(1)}, u32[]{:S(2)}, u32[]{:S(2)}) collective-permute-start(f32[256,128]{1,0:T(8,128)S(1)} %get-tuple-element.68), channel_id=1, source_target_pairs={{0,2},{1,3},{2,0},{3,1},{4,6},{5,7},{6,4},{7,5},{8,10},{9,11},{10,... | collective-permute-start | bytes 393224 | tf_op jit(solution)/shard_map/ppermute | solution.py:318
  26.7 9.0 %collective-permute-start.4 = (f32[256,128]{1,0:T(8,128)S(1)}, f32[256,128]{1,0:T(8,128)S(1)}, u32[]{:S(2)}, u32[]{:S(2)}) collective-permute-start(f32[256,128]{1,0:T(8,128)S(1)} %get-tuple-element.49), channel_id=1, source_target_pairs={{0,2},{1,3},{2,0},{3,1},{4,6},{5,7},{6,4},{7,5},{8,10},{9,11},{10,... | collective-permute-start | bytes 393224 | tf_op jit(solution)/shard_map/ppermute | solution.py:318
  28.6 7.1 %collective-permute-start.5 = (f32[256,128]{1,0:T(8,128)S(1)}, f32[256,128]{1,0:T(8,128)S(1)}, u32[]{:S(2)}, u32[]{:S(2)}) collective-permute-start(f32[256,128]{1,0:T(8,128)S(1)} %get-tuple-element.50), channel_id=1, source_target_pairs={{0,4},{1,5},{2,6},{3,7},{4,0},{5,1},{6,2},{7,3},{8,12},{9,13},{10,... | collective-permute-start | bytes 393224 | tf_op jit(solution)/shard_map/ppermute | solution.py:318
  30.1 5.9 %collective-permute-start.6 = (f32[256,128]{1,0:T(8,128)S(1)}, f32[256,128]{1,0:T(8,128)S(1)}, u32[]{:S(2)}, u32[]{:S(2)}) collective-permute-start(f32[256,128]{1,0:T(8,128)S(1)} %get-tuple-element.51), channel_id=1, source_target_pairs={{0,6},{1,7},{2,4},{3,5},{4,2},{5,3},{6,0},{7,1},{8,14},{9,15},{10,... | collective-permute-start | bytes 393224 | tf_op jit(solution)/shard_map/ppermute | solution.py:318
  30.5 14.8 %collective-permute-start.19 = (f32[256,128]{1,0:T(8,128)S(1)}, f32[256,128]{1,0:T(8,128)S(1)}, u32[]{:S(2)}, u32[]{:S(2)}) collective-permute-start(f32[256,128]{1,0:T(8,128)S(1)} %get-tuple-element.70), channel_id=1, source_target_pairs={{0,16},{1,17},{2,18},{3,19},{4,20},{5,21},{6,22},{7,23},{8,24},{9,... | collective-permute-start | bytes 393224 | tf_op jit(solution)/shard_map/ppermute | solution.py:318
  35.2 10.0 %collective-permute-start.20 = (f32[256,128]{1,0:T(8,128)S(1)}, f32[256,128]{1,0:T(8,128)S(1)}, u32[]{:S(2)}, u32[]{:S(2)}) collective-permute-start(f32[256,128]{1,0:T(8,128)S(1)} %get-tuple-element.71), channel_id=1, source_target_pairs={{0,24},{1,25},{2,26},{3,27},{4,28},{5,29},{6,30},{7,31},{8,16},{9,... | collective-permute-start | bytes 393224 | tf_op jit(solution)/shard_map/ppermute | solution.py:318
  36.2 10.7 %collective-permute-start.8 = (f32[256,128]{1,0:T(8,128)S(1)}, f32[256,128]{1,0:T(8,128)S(1)}, u32[]{:S(2)}, u32[]{:S(2)}) collective-permute-start(f32[256,128]{1,0:T(8,128)S(1)} %get-tuple-element.58), channel_id=1, source_target_pairs={{0,8},{1,9},{2,10},{3,11},{4,12},{5,13},{6,14},{7,15},{8,0},{9,1},... | collective-permute-start | bytes 393224 | tf_op jit(solution)/shard_map/ppermute | solution.py:318
  39.3 16.0 %collective-permute-start.9 = (f32[256,128]{1,0:T(8,128)S(1)}, f32[256,128]{1,0:T(8,128)S(1)}, u32[]{:S(2)}, u32[]{:S(2)}) collective-permute-start(f32[256,128]{1,0:T(8,128)S(1)} %get-tuple-element.59), channel_id=1, source_target_pairs={{0,16},{1,17},{2,18},{3,19},{4,20},{5,21},{6,22},{7,23},{8,24},{9,... | collective-permute-start | bytes 393224 | tf_op jit(solution)/shard_map/ppermute | solution.py:318
  41.3 14.0 %collective-permute-start.21 = (f32[256,128]{1,0:T(8,128)S(1)}, f32[256,128]{1,0:T(8,128)S(1)}, u32[]{:S(2)}, u32[]{:S(2)}) collective-permute-start(f32[256,128]{1,0:T(8,128)S(1)} %get-tuple-element.72), channel_id=1, source_target_pairs={{0,8},{1,9},{2,10},{3,11},{4,12},{5,13},{6,14},{7,15},{8,0},{9,1},... | collective-permute-start | bytes 393224 | tf_op jit(solution)/shard_map/ppermute | solution.py:318
  45.3 10.5 %collective-permute-start.22 = (f32[256,128]{1,0:T(8,128)S(1)}, f32[256,128]{1,0:T(8,128)S(1)}, u32[]{:S(2)}, u32[]{:S(2)}) collective-permute-start(f32[256,128]{1,0:T(8,128)S(1)} %get-tuple-element.69.refs_8_), channel_id=1, source_target_pairs={{0,1},{1,0},{2,3},{3,2},{4,5},{5,4},{6,7},{7,6},{8,9},{9,8},{10,11... | collective-permute-start | bytes 393224 | tf_op jit(solution)/shard_map/ppermute | solution.py:318
  45.3 10.5 %collective-permute-start.10 = (f32[256,128]{1,0:T(8,128)S(1)}, f32[256,128]{1,0:T(8,128)S(1)}, u32[]{:S(2)}, u32[]{:S(2)}) collective-permute-start(f32[256,128]{1,0:T(8,128)S(1)} %get-tuple-element.61), channel_id=1, source_target_pairs={{0,24},{1,25},{2,26},{3,27},{4,28},{5,29},{6,30},{7,31},{8,16},{9,... | collective-permute-start | bytes 393224 | tf_op jit(solution)/shard_map/ppermute | solution.py:318
  47.0 9.3 %collective-permute-start.23 = (f32[256,128]{1,0:T(8,128)S(1)}, f32[256,128]{1,0:T(8,128)S(1)}, u32[]{:S(2)}, u32[]{:S(2)}) collective-permute-start(f32[256,128]{1,0:T(8,128)S(1)} %collective-permute-done.19.refs_9_), channel_id=1, source_target_pairs={{0,1},{1,0},{2,3},{3,2},{4,5},{5,4},{6,7},{7,6},{8,9},{9,8},{10,11... | collective-permute-start | bytes 393224 | tf_op jit(solution)/shard_map/ppermute | solution.py:318
  55.2 2.1 %collective-permute-start.11 = (f32[256,128]{1,0:T(8,128)S(1)}, f32[256,128]{1,0:T(8,128)S(1)}, u32[]{:S(2)}, u32[]{:S(2)}) collective-permute-start(f32[256,128]{1,0:T(8,128)S(1)} %get-tuple-element.60.refs_0_), channel_id=1, source_target_pairs={{0,1},{1,0},{2,3},{3,2},{4,5},{5,4},{6,7},{7,6},{8,9},{9,8},{10,11... | collective-permute-start | bytes 393224 | tf_op jit(solution)/shard_map/ppermute | solution.py:318
  55.7 1.5 %collective-permute-start.14 = (f32[256,128]{1,0:T(8,128)S(1)}, f32[256,128]{1,0:T(8,128)S(1)}, u32[]{:S(2)}, u32[]{:S(2)}) collective-permute-start(f32[256,128]{1,0:T(8,128)S(1)} %collective-permute-done.8.refs_3_), channel_id=1, source_target_pairs={{0,1},{1,0},{2,3},{3,2},{4,5},{5,4},{6,7},{7,6},{8,9},{9,8},{10,11... | collective-permute-start | bytes 393224 | tf_op jit(solution)/shard_map/ppermute | solution.py:318
  55.8 1.5 %collective-permute-start.25 = (f32[256,128]{1,0:T(8,128)S(1)}, f32[256,128]{1,0:T(8,128)S(1)}, u32[]{:S(2)}, u32[]{:S(2)}) collective-permute-start(f32[256,128]{1,0:T(8,128)S(1)} %collective-permute-done.21.refs_11_), channel_id=1, source_target_pairs={{0,1},{1,0},{2,3},{3,2},{4,5},{5,4},{6,7},{7,6},{8,9},{9,8},{10,11... | collective-permute-start | bytes 393224 | tf_op jit(solution)/shard_map/ppermute | solution.py:318
  56.3 1.3 %collective-permute-start.12 = (f32[256,128]{1,0:T(8,128)S(1)}, f32[256,128]{1,0:T(8,128)S(1)}, u32[]{:S(2)}, u32[]{:S(2)}) collective-permute-start(f32[256,128]{1,0:T(8,128)S(1)} %collective-permute-done.9.refs_1_), channel_id=1, source_target_pairs={{0,1},{1,0},{2,3},{3,2},{4,5},{5,4},{6,7},{7,6},{8,9},{9,8},{10,11... | collective-permute-start | bytes 393224 | tf_op jit(solution)/shard_map/ppermute | solution.py:318
  (11 other events, 336.1 us)
